TPU v7x, 256 devices: a whole 4x4x8 slice. The times are simulated.
256 devices in a mesh: expert: 16 (over z, core), tensor: 16 (over y, x).
Axes of the slice: x: 4, y: 4, z: 8, core: 2. Of those that a mesh axis runs over, the one named last changes fastest.
Arguments:
- tokens: bfloat16 [32768, 4096], P(('expert', 'tensor')), may hold values from -6 to 6
- cotangent: bfloat16 [32768, 4096], P(('expert', 'tensor')), may hold values from -6 to 6
- expert_ids: int32 [32768, 1], P(('expert', 'tensor')), may hold values from 0 to 63; in each aligned block of 128 rows (0 to 127, 128 to 255, ...) at most 3 rows name the same one
- gate_values: bfloat16 [32768, 1], P(('expert', 'tensor')), may hold values from 0.049804688 to 0.5
- gate_weight: bfloat16 [256, 384, 4096], P(('expert', 'tensor')), may hold values from -0.09375 to 0.09375
- up_weight: bfloat16 [256, 384, 4096], P(('expert', 'tensor')), may hold values from -0.09375 to 0.09375
- down_weight: bfloat16 [256, 384, 4096], P(('expert', 'tensor')), may hold values from -0.15625 to 0.15625
Outputs:
- d_tokens: bfloat16 [32768, 4096], P(('expert', 'tensor'))
- gate_grad: bfloat16 [32768, 1], P(('expert', 'tensor'))
Inputs may be any that keep to these rules, and one draw needn't show every extreme that they name: `expert_ids`: each row names one expert. Among the rows of one device (aligned blocks of 128 tokens) no expert is named more than 3 times, a bound that some block reaches.
All inputs are finite; a program needn't handle non-finite values.
Results may differ from a plain program's by a relative error of at most 0.02.
Values may be sent and summed in bfloat16 or wider, within the bound.
A program may use at most 128 MiB of HBM per device.

v0:
```python
import jax
import jax.numpy as jnp
from jax import lax
from jax.sharding import PartitionSpec as P

SPLIT = 4


def expert_block(rows_all, rows_cot, rows_gate, w_gate, w_up, w_down):
    pre_gate = jnp.einsum("md,fd->mf", rows_all, w_gate, preferred_element_type=jnp.float32)
    pre_up = jnp.einsum("md,fd->mf", rows_all, w_up, preferred_element_type=jnp.float32)
    sigmoid_gate = jax.nn.sigmoid(pre_gate)
    swish_gate = pre_gate * sigmoid_gate
    hidden = (swish_gate * pre_up).astype(jnp.bfloat16)
    cot_proj = jnp.einsum("md,fd->mf", rows_cot, w_down, preferred_element_type=jnp.float32)
    gate_part = jnp.sum(hidden.astype(jnp.float32) * cot_proj, axis=1).astype(jnp.bfloat16)
    scaled = (rows_gate.astype(jnp.float32)[:, None] * rows_cot.astype(jnp.float32)).astype(
        jnp.bfloat16
    )
    d_hidden = jnp.einsum("md,fd->mf", scaled, w_down, preferred_element_type=jnp.float32)
    d_pre_gate = (
        d_hidden * pre_up * sigmoid_gate * (1.0 + pre_gate * (1.0 - sigmoid_gate))
    ).astype(jnp.bfloat16)
    d_pre_up = (d_hidden * swish_gate).astype(jnp.bfloat16)
    row_part = jnp.einsum("mf,fd->md", d_pre_gate, w_gate, preferred_element_type=jnp.float32)
    row_part = row_part + jnp.einsum(
        "mf,fd->md", d_pre_up, w_up, preferred_element_type=jnp.float32
    )
    return (row_part.astype(jnp.bfloat16), gate_part)


def local(tokens, cotangent, expert_ids, gate_values, gate_weight, up_weight, down_weight):
    groups = lax.axis_size("expert")
    tensor_count = lax.axis_size("tensor")
    tok_count, top_count = expert_ids.shape
    model_width = tokens.shape[1]
    per_group = tensor_count // SPLIT
    experts = groups * per_group
    capacity = min(tok_count, (3 * tok_count * top_count + 2 * experts - 1) // (2 * experts))
    route_count = tok_count * top_count
    slot_total = experts * capacity
    flat_ids = expert_ids.reshape(route_count)
    choose = (flat_ids[:, None] == jnp.arange(experts, dtype=jnp.int32)[None, :]).astype(jnp.int32)
    before = jnp.cumsum(choose, axis=0) - choose
    position = jnp.sum(before * choose, axis=1)
    owner_group = flat_ids // per_group
    local_slot = flat_ids % per_group
    target = (local_slot * groups + owner_group) * capacity + position
    slot_hits = (target[:, None] == jnp.arange(slot_total, dtype=jnp.int32)[None, :]).astype(
        jnp.int32
    )
    filled = jnp.sum(slot_hits, axis=0)
    route_index = jnp.arange(route_count, dtype=jnp.int32)
    source = jnp.where(filled > 0, jnp.sum(slot_hits * route_index[:, None], axis=0), route_count)
    token_pad = jnp.concatenate([tokens, jnp.zeros((1, model_width), jnp.bfloat16)], axis=0)
    cot_pad = jnp.concatenate([cotangent, jnp.zeros((1, model_width), jnp.bfloat16)], axis=0)
    gate_pad = jnp.concatenate(
        [gate_values.reshape(route_count), jnp.zeros((1,), jnp.bfloat16)], axis=0
    )
    token_row = source // top_count
    slot_rows = token_pad[token_row].reshape(per_group, groups, capacity, model_width)
    slot_cot = cot_pad[token_row].reshape(per_group, groups, capacity, model_width)
    slot_gates = gate_pad[source].reshape(per_group, groups, capacity)
    arrived_rows, arrived_cot, arrived_gates = (
        lax.all_to_all(slot_rows, "expert", split_axis=1, concat_axis=1, tiled=True),
        lax.all_to_all(slot_cot, "expert", split_axis=1, concat_axis=1, tiled=True),
        lax.all_to_all(slot_gates, "expert", split_axis=1, concat_axis=1, tiled=True),
    )
    copy_rows = jnp.repeat(arrived_rows, SPLIT, axis=0)
    copy_cot = jnp.repeat(arrived_cot, SPLIT, axis=0)
    copy_gates = jnp.repeat(arrived_gates, SPLIT, axis=0)
    rows_all, rows_cot, rows_gate = (
        lax.all_to_all(copy_rows, "tensor", split_axis=0, concat_axis=0, tiled=True),
        lax.all_to_all(copy_cot, "tensor", split_axis=0, concat_axis=0, tiled=True),
        lax.all_to_all(copy_gates, "tensor", split_axis=0, concat_axis=0, tiled=True),
    )
    many_rows = tensor_count * groups * capacity
    row_part, gate_part = expert_block(
        rows_all.reshape(many_rows, model_width),
        rows_cot.reshape(many_rows, model_width),
        rows_gate.reshape(many_rows),
        gate_weight[0],
        up_weight[0],
        down_weight[0],
    )
    row_part = row_part.reshape(tensor_count, groups, capacity, model_width)
    gate_part = gate_part.reshape(tensor_count, groups, capacity)
    back_parts, back_gates = (
        lax.all_to_all(row_part, "tensor", split_axis=0, concat_axis=0, tiled=True),
        lax.all_to_all(gate_part, "tensor", split_axis=0, concat_axis=0, tiled=True),
    )
    d_row = jnp.sum(
        back_parts.reshape(per_group, SPLIT, groups, capacity, model_width).astype(jnp.float32),
        axis=1,
    ).astype(jnp.bfloat16)
    gate_sum = jnp.sum(
        back_gates.reshape(per_group, SPLIT, groups, capacity).astype(jnp.float32), axis=1
    ).astype(jnp.bfloat16)
    home_rows, home_gates = (
        lax.all_to_all(d_row, "expert", split_axis=1, concat_axis=1, tiled=True),
        lax.all_to_all(gate_sum, "expert", split_axis=1, concat_axis=1, tiled=True),
    )
    per_route = home_rows.reshape(slot_total, model_width)[target]
    d_tokens = jnp.sum(
        per_route.astype(jnp.float32).reshape(tok_count, top_count, model_width), axis=1
    ).astype(jnp.bfloat16)
    gate_grad = home_gates.reshape(slot_total)[target].reshape(tok_count, top_count)
    return (d_tokens, gate_grad)


def solution(mesh):
    placed = (
        P(("expert", "tensor"), None),
        P(("expert", "tensor"), None),
        P(("expert", "tensor"), None),
        P(("expert", "tensor"), None),
        P(("expert", "tensor"), None, None),
        P(("expert", "tensor"), None, None),
        P(("expert", "tensor"), None, None),
    )
    return jax.shard_map(
        local,
        mesh=mesh,
        in_specs=placed,
        out_specs=(P(("expert", "tensor"), None), P(("expert", "tensor"), None)),
        check_vma=False,
    )
```

profile of v0, /device:TPU:1, one launch (start us, length us, event | category | flops | bytes accessed | tf_op | source)
XLA Modules:
  0.0 631.3 jit_solution(8302376098684809635)
XLA Ops:
  5.8 17.1 %all_to_all.50 = bf16[4,16,3]{2,0,1:T(4,128)(2,1)S(1)} all-to-all(bf16[4,16,3]{2,0,1:T(4,128)(2,1)S(1)} %copy.61), channel_id=1, replica_groups=mesh['expert'=16,'tensor'=16] {'expert'}, dimensions={1} | all-to-all | bytes 768 | tf_op jit(solution)/shard_map/all_to_all | solution.py:67
  23.6 6.8 %all-to-all-start.1 = ((bf16[16,16,3]{1,2,0:T(4,128)(2,1)}), bf16[16,16,3]{1,2,0:T(4,128)(2,1)S(1)}, u32[]{:S(2)}, u32[]{:S(2)}) async-start(bf16[16,16,3]{1,2,0:T(4,128)(2,1)} %bitcast.6), calls=%async_computation.1 | async-start | bytes 32768 | tf_op jit(solution)/shard_map/all_to_all | solution.py:75
  30.4 2.3 concatenate.11
  32.7 5.6 gather_fusion.2
  38.3 4.1 reshape.108
  42.4 4.9 copy.66
  47.3 4.8 all-to-all-start.4
  52.1 2.3 concatenate.10
  54.4 5.6 gather_fusion.1
  60.1 4.1 reshape.106
  64.1 4.9 copy.63
  69.1 21.6 %all-to-all-done.4 = bf16[4,16,3,4096]{3,0,2,1:T(4,128)(2,1)} async-done(((bf16[4,16,3,4096]{3,0,2,1:T(4,128)(2,1)}), bf16[4,16,3,4096]{3,0,2,1:T(4,128)(2,1)}, u32[]{:S(2)}, u32[]{:S(2)}) %all-to-all-start.4) | async-done | bytes 1572896 | tf_op jit(solution)/shard_map/all_to_all | solution.py:65
  90.7 4.6 all-to-all-start.2
  95.3 3.4 copy.67
  98.7 34.9 %all-to-all-done.2 = bf16[4,16,3,4096]{3,0,2,1:T(4,128)(2,1)} async-done(((bf16[4,16,3,4096]{3,0,2,1:T(4,128)(2,1)}), bf16[4,16,3,4096]{3,0,2,1:T(4,128)(2,1)}, u32[]{:S(2)}, u32[]{:S(2)}) %all-to-all-start.2) | async-done | bytes 1572896 | tf_op jit(solution)/shard_map/all_to_all | solution.py:66
  133.7 4.8 broadcast_in_dim.13
  138.5 7.0 %all-to-all-start.5 = ((bf16[16,16,3,4096]{3,1,2,0:T(8,128)(2,1)}), bf16[16,16,3,4096]{3,1,2,0:T(8,128)(2,1)}, u32[]{:S(2)}, u32[]{:S(2)}) async-start(bf16[16,16,3,4096]{3,1,2,0:T(8,128)(2,1)} %bitcast.42), calls=%async_computation.5 | async-start | bytes 12582912 | tf_op jit(solution)/shard_map/all_to_all | solution.py:73
  145.5 3.5 copy.64
  149.0 93.7 %all-to-all-done.5 = bf16[16,16,3,4096]{3,1,2,0:T(8,128)(2,1)} async-done(((bf16[16,16,3,4096]{3,1,2,0:T(8,128)(2,1)}), bf16[16,16,3,4096]{3,1,2,0:T(8,128)(2,1)}, u32[]{:S(2)}, u32[]{:S(2)}) %all-to-all-start.5) | async-done | bytes 6291488 | tf_op jit(solution)/shard_map/all_to_all | solution.py:73
  242.7 4.8 broadcast_in_dim.12
  247.4 4.7 all-to-all-start.3
  252.1 11.5 %copy.68 = bf16[16,16,3,4096]{3,2,1,0:T(4,128)(2,1)} copy(bf16[16,16,3,4096]{3,1,2,0:T(8,128)(2,1)} %all-to-all-done.5) | data formatting | bytes 12582912 | tf_op jit(solution)/shard_map/all_to_all | solution.py:73
  263.6 13.6 %reshape.110 = bf16[768,4096]{1,0:T(8,128)(2,1)} reshape(bf16[16,16,3,4096]{3,2,1,0:T(4,128)(2,1)} %copy.68) | data formatting | bytes 12582912 | tf_op jit(solution)/shard_map/reshape | solution.py:79
  277.3 7.1 %fusion.2 = f32[768,384]{1,0:T(8,128)} fusion(bf16[768,4096]{1,0:T(8,128)(2,1)} %reshape.110, bf16[1,384,4096]{2,1,0:T(8,128)(2,1)S(1)} %copy-done), kind=kOutput, calls=%fused_computation.10 | convolution fusion | flops 2415919104 | bytes 10616832 | tf_op jit(solution)/shard_map/md,fd->mf/dot_general | solution.py:10
  284.4 4.4 fusion.5
  288.8 56.5 %all-to-all-done.3 = bf16[16,16,3,4096]{3,1,2,0:T(8,128)(2,1)} async-done(((bf16[16,16,3,4096]{3,1,2,0:T(8,128)(2,1)}), bf16[16,16,3,4096]{3,1,2,0:T(8,128)(2,1)}, u32[]{:S(2)}, u32[]{:S(2)}) %all-to-all-start.3) | async-done | bytes 6291488 | tf_op jit(solution)/shard_map/all_to_all | solution.py:74
  345.4 11.5 %copy.77 = bf16[16,16,3,4096]{3,2,1,0:T(4,128)(2,1)} copy(bf16[16,16,3,4096]{3,1,2,0:T(8,128)(2,1)} %all-to-all-done.3) | data formatting | bytes 12582912 | tf_op jit(solution)/shard_map/all_to_all | solution.py:74
  356.9 13.7 %reshape.114 = bf16[768,4096]{1,0:T(8,128)(2,1)} reshape(bf16[16,16,3,4096]{3,2,1,0:T(4,128)(2,1)} %copy.77) | data formatting | bytes 12582912 | tf_op jit(solution)/shard_map/reshape | solution.py:80
  370.6 7.9 %fusion.14 = bf16[768]{0:T(1024)(128)(2,1)S(1)} fusion(bf16[768,4096]{1,0:T(8,128)(2,1)} %reshape.114, bf16[1,384,4096]{2,1,0:T(8,128)(2,1)} %param.13, f32[768,384]{1,0:T(8,128)} %fusion.5, f32[768,384]{1,0:T(8,128)} %fusion.2), kind=kOutput, calls=%fused_computation.20 | convolution fusion | flops 2418572544 | bytes 11798016 | tf_op jit(solution)/shard_map/md,fd->mf/dot_general | solution.py:15
  379.5 5.0 all-to-all-start.8
  384.5 7.6 %multiply_convert_fusion = bf16[16,16,3,4096]{3,1,2,0:T(8,128)(2,1)} fusion(bf16[16,16,3,4096]{3,1,2,0:T(8,128)(2,1)} %all-to-all-done.3, f32[16,16,3]{1,2,0:T(4,128)S(1)} %convert_element_type.55), kind=kLoop, calls=%fused_computation.6 | loop fusion | flops 9437184 | bytes 12585984 | tf_op jit(solution)/shard_map/convert_element_type | solution.py:17
  392.1 11.5 %copy.65 = bf16[16,16,3,4096]{3,2,1,0:T(4,128)(2,1)} copy(bf16[16,16,3,4096]{3,1,2,0:T(8,128)(2,1)} %multiply_convert_fusion) | data formatting | bytes 12582912 | tf_op jit(solution)/shard_map/convert_element_type | solution.py:17
  403.6 13.7 %convert_element_type.58 = bf16[768,4096]{1,0:T(8,128)(2,1)} reshape(bf16[16,16,3,4096]{3,2,1,0:T(4,128)(2,1)} %copy.65) | data formatting | bytes 12582912 | tf_op jit(solution)/shard_map/convert_element_type | solution.py:17
  417.4 6.8 %fusion.9 = f32[768,384]{1,0:T(8,128)S(1)} fusion(bf16[768,4096]{1,0:T(8,128)(2,1)} %convert_element_type.58, bf16[1,384,4096]{2,1,0:T(8,128)(2,1)} %param.13), kind=kOutput, calls=%fused_computation.17 | convolution fusion | flops 2415919104 | bytes 10616832 | tf_op jit(solution)/shard_map/md,fd->mf/dot_general | solution.py:20
  425.3 3.7 fusion
  429.0 8.5 %add_convert_fusion = bf16[768,4096]{1,0:T(8,128)(2,1)} fusion(f32[768,4096]{1,0:T(8,128)S(1)} %fusion, bf16[1,384,4096]{2,1,0:T(8,128)(2,1)} %param.12, f32[768,384]{1,0:T(8,128)} %copy-done.2, f32[768,384]{1,0:T(8,128)S(1)} %copy-done.1), kind=kOutput, calls=%fused_computation.5 | convolution fusion | flops 2423980032 | bytes 24379392 | tf_op jit(solution)/shard_map/mf,fd->md/dot_general | solution.py:26
  437.4 12.9 %reshape.111 = bf16[16,16,3,4096]{3,2,1,0:T(4,128)(2,1)} reshape(bf16[768,4096]{1,0:T(8,128)(2,1)} %add_convert_fusion) | data formatting | bytes 12582912 | tf_op jit(solution)/shard_map/reshape | solution.py:86
  450.4 11.2 %copy.73 = bf16[16,16,3,4096]{3,1,2,0:T(8,128)(2,1)} copy(bf16[16,16,3,4096]{3,2,1,0:T(4,128)(2,1)} %reshape.111) | data formatting | bytes 12582912 | tf_op jit(solution)/shard_map/reshape | solution.py:86
  461.5 6.8 %all-to-all-start.6 = ((bf16[16,16,3,4096]{3,1,2,0:T(8,128)(2,1)}), bf16[16,16,3,4096]{3,1,2,0:T(8,128)(2,1)}, u32[]{:S(2)}, u32[]{:S(2)}) async-start(bf16[16,16,3,4096]{3,1,2,0:T(8,128)(2,1)} %copy.73), calls=%async_computation.6 | async-start | bytes 12582912 | tf_op jit(solution)/shard_map/all_to_all | solution.py:89
  469.1 89.1 %all-to-all-done.6 = bf16[16,16,3,4096]{3,1,2,0:T(8,128)(2,1)} async-done(((bf16[16,16,3,4096]{3,1,2,0:T(8,128)(2,1)}), bf16[16,16,3,4096]{3,1,2,0:T(8,128)(2,1)}, u32[]{:S(2)}, u32[]{:S(2)}) %all-to-all-start.6) | async-done | bytes 6291488 | tf_op jit(solution)/shard_map/all_to_all | solution.py:89
  558.2 6.8 %all-to-all-start.9 = ((bf16[4,16,3]{2,0,1:T(4,128)(2,1)}), bf16[4,16,3]{2,0,1:T(4,128)(2,1)S(1)}, u32[]{:S(2)}, u32[]{:S(2)}) async-start(bf16[4,16,3]{2,0,1:T(4,128)(2,1)} %copy.80), calls=%async_computation.9 | async-start | bytes 32768 | tf_op jit(solution)/shard_map/all_to_all | solution.py:101
  565.0 4.1 bitcast_reduce_fusion
  569.1 2.4 copy.74
  572.3 6.5 %all-to-all-start.7 = ((bf16[4,16,3,4096]{3,0,2,1:T(4,128)(2,1)}), bf16[4,16,3,4096]{3,0,2,1:T(4,128)(2,1)}, u32[]{:S(2)}, u32[]{:S(2)}) async-start(bf16[4,16,3,4096]{3,0,2,1:T(4,128)(2,1)} %copy.74), calls=%async_computation.7 | async-start | bytes 3145728 | tf_op jit(solution)/shard_map/all_to_all | solution.py:100
  580.7 36.6 %all-to-all-done.7 = bf16[4,16,3,4096]{3,0,2,1:T(4,128)(2,1)} async-done(((bf16[4,16,3,4096]{3,0,2,1:T(4,128)(2,1)}), bf16[4,16,3,4096]{3,0,2,1:T(4,128)(2,1)}, u32[]{:S(2)}, u32[]{:S(2)}) %all-to-all-start.7) | async-done | bytes 1572896 | tf_op jit(solution)/shard_map/all_to_all | solution.py:100
  617.3 4.4 copy.75
  621.8 4.3 reshape.113
  626.0 4.8 gather_fusion.3
  (38 shorter events, 11.3 us)
Async XLA Ops:
  0.6 276.6 %copy-start = (bf16[1,384,4096]{2,1,0:T(8,128)(2,1)S(1)}, bf16[1,384,4096]{2,1,0:T(8,128)(2,1)}, u32[]{:S(2)}) copy-start(bf16[1,384,4096]{2,1,0:T(8,128)(2,1)} %param.11) | copy-start | bytes 9437188
  23.6 23.6 %all-to-all-start.1 = ((bf16[16,16,3]{1,2,0:T(4,128)(2,1)}), bf16[16,16,3]{1,2,0:T(4,128)(2,1)S(1)}, u32[]{:S(2)}, u32[]{:S(2)}) async-start(bf16[16,16,3]{1,2,0:T(4,128)(2,1)} %bitcast.6), calls=%async_computation.1 | async-start | bytes 32768 | tf_op jit(solution)/shard_map/all_to_all | solution.py:75
  47.3 43.4 %all-to-all-start.4 = ((bf16[4,16,3,4096]{3,0,2,1:T(4,128)(2,1)}), bf16[4,16,3,4096]{3,0,2,1:T(4,128)(2,1)}, u32[]{:S(2)}, u32[]{:S(2)}) async-start(bf16[4,16,3,4096]{3,0,2,1:T(4,128)(2,1)} %copy.66), calls=%async_computation.4 | async-start | bytes 3145728 | tf_op jit(solution)/shard_map/all_to_all | solution.py:65
  90.7 43.0 %all-to-all-start.2 = ((bf16[4,16,3,4096]{3,0,2,1:T(4,128)(2,1)}), bf16[4,16,3,4096]{3,0,2,1:T(4,128)(2,1)}, u32[]{:S(2)}, u32[]{:S(2)}) async-start(bf16[4,16,3,4096]{3,0,2,1:T(4,128)(2,1)} %copy.63), calls=%async_computation.2 | async-start | bytes 3145728 | tf_op jit(solution)/shard_map/all_to_all | solution.py:66
  138.5 104.1 %all-to-all-start.5 = ((bf16[16,16,3,4096]{3,1,2,0:T(8,128)(2,1)}), bf16[16,16,3,4096]{3,1,2,0:T(8,128)(2,1)}, u32[]{:S(2)}, u32[]{:S(2)}) async-start(bf16[16,16,3,4096]{3,1,2,0:T(8,128)(2,1)} %bitcast.42), calls=%async_computation.5 | async-start | bytes 12582912 | tf_op jit(solution)/shard_map/all_to_all | solution.py:73
  247.4 97.9 %all-to-all-start.3 = ((bf16[16,16,3,4096]{3,1,2,0:T(8,128)(2,1)}), bf16[16,16,3,4096]{3,1,2,0:T(8,128)(2,1)}, u32[]{:S(2)}, u32[]{:S(2)}) async-start(bf16[16,16,3,4096]{3,1,2,0:T(8,128)(2,1)} %bitcast.41), calls=%async_computation.3 | async-start | bytes 12582912 | tf_op jit(solution)/shard_map/all_to_all | solution.py:74
  277.3 7.1 %copy-start.3 = (bf16[768,4096]{1,0:T(8,128)(2,1)S(1)}, bf16[768,4096]{1,0:T(8,128)(2,1)}, u32[]{:S(2)}) copy-start(bf16[768,4096]{1,0:T(8,128)(2,1)} %reshape.110) | copy-start | bytes 18874372
  277.3 7.1 %copy-start.4 = (bf16[1,384,4096]{2,1,0:T(8,128)(2,1)S(1)}, bf16[1,384,4096]{2,1,0:T(8,128)(2,1)}, u32[]{:S(2)}) copy-start(bf16[1,384,4096]{2,1,0:T(8,128)(2,1)} %param.12) | copy-start | bytes 9437188
  379.5 82.0 %all-to-all-start.8 = ((bf16[16,16,3]{1,2,0:T(4,128)(2,1)}), bf16[16,16,3]{1,2,0:T(4,128)(2,1)S(1)}, u32[]{:S(2)}, u32[]{:S(2)}) async-start(bf16[16,16,3]{1,2,0:T(4,128)(2,1)} %copy.79), calls=%async_computation.8 | async-start | bytes 32768 | tf_op jit(solution)/shard_map/all_to_all | solution.py:90
  417.4 7.9 %copy-start.1 = (f32[768,384]{1,0:T(8,128)S(1)}, f32[768,384]{1,0:T(8,128)}, u32[]{:S(2)}) copy-start(f32[768,384]{1,0:T(8,128)} %fusion.2) | copy-start | bytes 3538948
  417.4 7.9 %copy-start.5 = (f32[768,384]{1,0:T(8,128)S(1)}, f32[768,384]{1,0:T(8,128)}, u32[]{:S(2)}) copy-start(f32[768,384]{1,0:T(8,128)} %fusion.5) | copy-start | bytes 3538948
  424.2 1.1 copy-start.2
  461.5 96.7 %all-to-all-start.6 = ((bf16[16,16,3,4096]{3,1,2,0:T(8,128)(2,1)}), bf16[16,16,3,4096]{3,1,2,0:T(8,128)(2,1)}, u32[]{:S(2)}, u32[]{:S(2)}) async-start(bf16[16,16,3,4096]{3,1,2,0:T(8,128)(2,1)} %copy.73), calls=%async_computation.6 | async-start | bytes 12582912 | tf_op jit(solution)/shard_map/all_to_all | solution.py:89
  558.2 14.1 %all-to-all-start.9 = ((bf16[4,16,3]{2,0,1:T(4,128)(2,1)}), bf16[4,16,3]{2,0,1:T(4,128)(2,1)S(1)}, u32[]{:S(2)}, u32[]{:S(2)}) async-start(bf16[4,16,3]{2,0,1:T(4,128)(2,1)} %copy.80), calls=%async_computation.9 | async-start | bytes 32768 | tf_op jit(solution)/shard_map/all_to_all | solution.py:101
  572.3 45.0 %all-to-all-start.7 = ((bf16[4,16,3,4096]{3,0,2,1:T(4,128)(2,1)}), bf16[4,16,3,4096]{3,0,2,1:T(4,128)(2,1)}, u32[]{:S(2)}, u32[]{:S(2)}) async-start(bf16[4,16,3,4096]{3,0,2,1:T(4,128)(2,1)} %copy.74), calls=%async_computation.7 | async-start | bytes 3145728 | tf_op jit(solution)/shard_map/all_to_all | solution.py:100
where the time goes:
time: 642 us; the launch traced here: 631 us
  waiting for transfers between devices  333 us (52%)
  local copies, waits for them, and re-layouts  173 us (27%)
  starting transfers between devices  53 us (8%)
  matrix products  38.5 us (6%)
  blocking collectives  17.1 us (3%)
  other arithmetic  15.2 us (2%)
    all_to_all x1, waiting for transfers between devices, local(): lax.all_to_all(copy_rows, 'tensor', split_axis=0, concat_axis=0, tiled=True)  93.7 us
    all_to_all x1, waiting for transfers between devices, local(): lax.all_to_all(row_part, 'tensor', split_axis=0, concat_axis=0, tiled=True)  89.1 us
    all_to_all x1, waiting for transfers between devices, local(): lax.all_to_all(copy_cot, 'tensor', split_axis=0, concat_axis=0, tiled=True)  56.5 us
    all_to_all x1, waiting for transfers between devices, local(): lax.all_to_all(d_row, 'expert', split_axis=1, concat_axis=1, tiled=True)  36.6 us
    all_to_all x1, waiting for transfers between devices, local(): lax.all_to_all(slot_cot, 'expert', split_axis=1, concat_axis=1, tiled=True)  34.9 us
    convert_element_type x2, local copies, waits for them, and re-layouts, expert_block(): (rows_gate.astype(jnp.float32)[:, None] * rows_cot.astype(jnp.float32)).a...  25.3 us
    reshape x2, local copies, waits for them, and re-layouts, local(): row_part = row_part.reshape(tensor_count, groups, capacity, model_width)  24.1 us
    all_to_all x1, waiting for transfers between devices, local(): lax.all_to_all(slot_rows, 'expert', split_axis=1, concat_axis=1, tiled=True)  21.6 us
  transfers between devices with their start and end apart: 9, of which 7 were waited for; matrix products, arithmetic and copies ran while one was open for 26% of the time, Pallas kernels for 0%

commit v1 on v0

v1 whole, which is shorter than its diff:
```python
import functools

import jax
import jax.numpy as jnp
from jax import lax
from jax.experimental import pallas as pl
from jax.experimental.pallas import tpu as pltpu
from jax.sharding import PartitionSpec as P

MESH = pl.DeviceIdType.MESH
BF = jnp.bfloat16
F32 = jnp.float32

D = 4096
HID = 384
TOK = 128
CAP = 3
NZ, NY, NC, NX = 8, 4, 2, 4
PEERS = NZ * NY * NC
SLOTS = PEERS * CAP
CHUNKS = 4
PER = PEERS // CHUNKS
ROWS = PER * CAP
MANY = ROWS * NX
LANES = 128
SUB = D // LANES
WIDE = D + LANES
HALF = D // 2
BACK = CAP * SUB + 16
ZORD = (0, 1, 6, 3, 5, 4, 7, 2)
NT = (((1,), (1,)), ((), ()))


def kernel(
    tok_hbm,
    cot_hbm,
    ids_ref,
    gate_ref,
    wg_hbm,
    wu_hbm,
    wd_hbm,
    dtok_hbm,
    ggrad_ref,
    src,
    wts,
    out_rows,
    in_rows,
    xrows,
    pre,
    part,
    relay,
    full,
    ret_out,
    ret_in,
    home,
    dtok,
    load_sem,
    w_sem,
    disp_send,
    disp_recv,
    ag_send,
    ag_recv,
    rs_send,
    rs_recv,
    ret_send,
    ret_recv,
    out_sem,
):
    expert = lax.axis_index("expert")
    tensor = lax.axis_index("tensor")
    mz, mc = expert // NC, expert % NC
    my, mx = tensor // NX, tensor % NX

    def device(z, c, y, x):
        return (z * NC + c, y * NX + x)

    def peer(sign, kz, j):
        ky, kc = j // NC, j % NC
        return device(
            lax.rem(mz + sign * kz + NZ, NZ),
            lax.rem(mc + kc, NC),
            lax.rem(my + sign * ky + NY, NY),
            mx,
        )

    right = device(mz, mc, my, lax.rem(mx + 1, NX))
    left = device(mz, mc, my, lax.rem(mx + NX - 1, NX))

    loads = [
        pltpu.make_async_copy(tok_hbm, src.at[0], load_sem.at[0]),
        pltpu.make_async_copy(cot_hbm, src.at[1], load_sem.at[1]),
    ]
    weight_loads = [
        pltpu.make_async_copy(w.at[0], wts.at[i], w_sem.at[i])
        for i, w in enumerate((wg_hbm, wu_hbm, wd_hbm))
    ]
    for copy in loads + weight_loads:
        copy.start()

    barrier = pltpu.get_barrier_semaphore()
    for q in range(NZ):

        def greet(j, carry, q=q):
            pl.semaphore_signal(
                barrier, inc=1, device_id=peer(1, ZORD[q], j), device_id_type=MESH
            )
            return carry

        lax.fori_loop(1 if q == 0 else 0, NY * NC, greet, 0)
    for neighbour in (left, right):
        pl.semaphore_signal(barrier, inc=1, device_id=neighbour, device_id_type=MESH)

    ids = ids_ref[...]
    t0 = lax.broadcasted_iota(jnp.int32, (TOK, TOK), 0)
    t1 = lax.broadcasted_iota(jnp.int32, (TOK, TOK), 1)
    ids_row = jnp.sum(jnp.where(t0 == t1, ids, 0), axis=0, keepdims=True)
    earlier = jnp.where((ids == ids_row) & (t1 < t0), 1, 0)
    position = jnp.sum(earlier, axis=1, keepdims=True)
    kz = ((ids >> 3) - mz) & (NZ - 1)
    kc = ((ids >> 2) - mc) & (NC - 1)
    ky = (ids - my) & (NY - 1)
    q_of = jnp.zeros_like(kz)
    for q in range(NZ):
        q_of = jnp.where(kz == ZORD[q], q, q_of)
    peer_of = (q_of * NY + ky) * NC + kc
    slot = peer_of * CAP + position
    slot_row = jnp.sum(jnp.where(t0 == t1, slot, 0), axis=0, keepdims=True)
    gate = gate_ref[...].astype(F32)

    def sort(c, h):
        at = lax.broadcasted_iota(jnp.int32, (ROWS, TOK), 0) + c * ROWS
        pick = jnp.where(at == slot_row, 1.0, 0.0).astype(BF)
        for j in range(0, D, 2048):
            rows = jnp.dot(pick, src[h, :, j : j + 2048], preferred_element_type=F32)
            out_rows[h, pl.ds(c * ROWS, ROWS), j // LANES : (j + 2048) // LANES, :] = (
                pltpu.einshape("a(bc)->abc", rows.astype(BF), c=LANES)
            )

    def dispatch(c, h):
        for q in range(c * NZ // CHUNKS, (c + 1) * NZ // CHUNKS):

            def send(j, carry, q=q):
                at = pl.ds((q * NY * NC + j) * CAP, CAP)
                pltpu.make_async_remote_copy(
                    src_ref=out_rows.at[h, at],
                    dst_ref=in_rows.at[h, at],
                    send_sem=disp_send.at[h, c],
                    recv_sem=disp_recv.at[h, c],
                    device_id=peer(1, ZORD[q], j),
                    device_id_type=MESH,
                ).start()
                return carry

            lax.fori_loop(1 if q == 0 else 0, NY * NC, send, 0)

    def remote_slots(c):
        skip = CAP if c == 0 else 0
        return pl.ds(c * ROWS + skip, ROWS - skip)

    def gather_copy(c, h, kind):
        x = xrows.at[h, c]
        own, from_left, far, from_right = (pl.ds(i * ROWS, ROWS) for i in range(4))
        a, b = pl.ds(0, HALF), pl.ds(HALF, HALF)
        ref_pair, to = (
            ((x.at[own], x.at[from_left]), right),
            ((x.at[own], x.at[from_right]), left),
            ((x.at[from_left, a], x.at[far, a]), right),
            ((x.at[from_right, b], x.at[far, b]), left),
        )[kind]
        return pltpu.make_async_remote_copy(
            src_ref=ref_pair[0],
            dst_ref=ref_pair[1],
            send_sem=ag_send.at[h, c, kind],
            recv_sem=ag_recv.at[h, c, kind],
            device_id=to,
            device_id_type=MESH,
        )

    def arrive(c, h):
        at = remote_slots(c)
        pltpu.make_async_copy(
            out_rows.at[h, at], in_rows.at[h, at], disp_recv.at[h, c]
        ).wait()
        if c == 0:
            in_rows[h, 0:CAP] = out_rows[h, 0:CAP]
        for j in range(0, SUB, 16):
            xrows[h, c, 0:ROWS, j * LANES : (j + 16) * LANES] = pltpu.einshape(
                "abc->a(bc)", in_rows[h, pl.ds(c * ROWS, ROWS), j : j + 16, :]
            )
        gather_copy(c, h, 0).start()
        gather_copy(c, h, 1).start()

    def forward(c, h):
        gather_copy(c, h, 0).wait_recv()
        gather_copy(c, h, 2).start()
        gather_copy(c, h, 1).wait_recv()
        gather_copy(c, h, 3).start()

    def compute(c, h):
        gather_copy(c, h, 2).wait_recv()
        gather_copy(c, h, 3).wait_recv()
        if h == 0:
            if c == 0:
                weight_loads[0].wait()
                weight_loads[1].wait()
            pre[0] = lax.dot_general(
                xrows[0, c], wts[0], NT, preferred_element_type=F32
            )
            pre[1] = lax.dot_general(
                xrows[0, c], wts[1], NT, preferred_element_type=F32
            )
            return
        if c == 0:
            weight_loads[2].wait()
        d_hidden = lax.dot_general(
            xrows[1, c], wts[2], NT, preferred_element_type=F32
        )
        pre_gate, pre_up = pre[0], pre[1]
        sigmoid_gate = jax.nn.sigmoid(pre_gate)
        swish_gate = pre_gate * sigmoid_gate
        hidden = (swish_gate * pre_up).astype(BF).astype(F32)
        gate_part = jnp.sum(hidden * d_hidden, axis=1, keepdims=True)
        part[c, :, D:WIDE] = jnp.broadcast_to(gate_part, (MANY, LANES)).astype(BF)
        d_gate = (
            d_hidden * pre_up * sigmoid_gate * (1.0 + pre_gate * (1.0 - sigmoid_gate))
        ).astype(BF)
        d_up = (d_hidden * swish_gate).astype(BF)
        for j in range(0, D, 512):
            if j == HALF:
                scatter_copy(c, 0).start()
                scatter_copy(c, 3).start()
            at = slice(j, j + 512)
            part[c, :, at] = (
                jnp.dot(d_gate, wts[0, :, at], preferred_element_type=F32)
                + jnp.dot(d_up, wts[1, :, at], preferred_element_type=F32)
            ).astype(BF)
        scatter_copy(c, 1).start()
        scatter_copy(c, 2).start()

    def scatter_copy(c, kind):
        p = part.at[c]
        from_left_rows, far, from_right_rows = (pl.ds(i * ROWS, ROWS) for i in (1, 2, 3))
        a, b = pl.ds(0, HALF), pl.ds(HALF, WIDE - HALF)
        ref_pair, to = (
            ((p.at[far, a], relay.at[c, :, a]), right),
            ((p.at[far, b], relay.at[c, :, b]), left),
            ((p.at[from_right_rows, b], full.at[c, 0, :, b]), right),
            ((p.at[from_left_rows, a], full.at[c, 1, :, a]), left),
            ((p.at[from_right_rows, a], full.at[c, 0, :, a]), right),
            ((p.at[from_left_rows, b], full.at[c, 1, :, b]), left),
        )[kind]
        return pltpu.make_async_remote_copy(
            src_ref=ref_pair[0],
            dst_ref=ref_pair[1],
            send_sem=rs_send.at[c, kind],
            recv_sem=rs_recv.at[c, kind],
            device_id=to,
            device_id_type=MESH,
        )

    def pass_on(c):
        for kind, rows, cols in (
            (0, slice(3 * ROWS, 4 * ROWS), slice(0, HALF)),
            (1, slice(ROWS, 2 * ROWS), slice(HALF, WIDE)),
        ):
            scatter_copy(c, kind).wait_recv()
            part[c, rows, cols] = (
                part[c, rows, cols].astype(F32) + relay[c, :, cols].astype(F32)
            ).astype(BF)
            scatter_copy(c, kind + 4).start()

    def send_home(c):
        for kind in (2, 3, 4, 5):
            scatter_copy(c, kind).wait_recv()

        def total(at):
            return (
                part[c, 0:ROWS, at].astype(F32)
                + full[c, 0, :, at].astype(F32)
                + full[c, 1, :, at].astype(F32)
            ).astype(BF)

        for j in range(0, D, 2048):
            tiles = pltpu.einshape("a(bc)->abc", total(slice(j, j + 2048)), c=LANES)
            for i in range(PER):
                for p in range(CAP):
                    at = p * SUB + j // LANES
                    ret_out[c * PER + i, at : at + 16, :] = tiles[i * CAP + p]
        r0 = lax.broadcasted_iota(jnp.int32, (PER * 16, ROWS), 0)
        r1 = lax.broadcasted_iota(jnp.int32, (PER * 16, ROWS), 1)
        spread = jnp.where(
            (r1 == (r0 >> 4) * CAP + (r0 & 15)) & ((r0 & 15) < CAP), 1.0, 0.0
        ).astype(BF)
        gates = jnp.dot(spread, total(slice(D, WIDE)), preferred_element_type=F32)
        ret_out[c * PER : (c + 1) * PER, CAP * SUB : BACK, :] = gates.astype(BF).reshape(
            PER, 16, LANES
        )
        for q in range(c * NZ // CHUNKS, (c + 1) * NZ // CHUNKS):

            def send(j, carry, q=q):
                at = q * NY * NC + j
                pltpu.make_async_remote_copy(
                    src_ref=ret_out.at[at],
                    dst_ref=ret_in.at[at],
                    send_sem=ret_send.at[c],
                    recv_sem=ret_recv.at[c],
                    device_id=peer(-1, ZORD[q], j),
                    device_id_type=MESH,
                ).start()
                return carry

            lax.fori_loop(1 if q == 0 else 0, NY * NC, send, 0)
        if c == 0:
            ret_in[0] = ret_out[0]

    def returned(c):
        skip = 1 if c == 0 else 0
        return pl.ds(c * PER + skip, PER - skip)

    def come_home(c):
        at = returned(c)
        pltpu.make_async_copy(ret_out.at[at], ret_in.at[at], ret_recv.at[c]).wait()
        rows = ret_in[c * PER : (c + 1) * PER, 0 : CAP * SUB, :].reshape(
            ROWS, SUB, LANES
        )
        for j in range(0, SUB, 16):
            home[c * ROWS : (c + 1) * ROWS, j * LANES : (j + 16) * LANES] = (
                pltpu.einshape("abc->a(bc)", rows[:, j : j + 16, :])
            )

    def finish():
        at = lax.broadcasted_iota(jnp.int32, (TOK, SLOTS), 1)
        pick = jnp.where(at == slot, 1.0, 0.0).astype(BF)
        for j in range(0, D, 1024):
            dtok[:, j : j + 1024] = jnp.dot(
                pick, home[:, j : j + 1024], preferred_element_type=F32
            ).astype(BF)
        out = pltpu.make_async_copy(dtok, dtok_hbm, out_sem)
        out.start()
        at = lax.broadcasted_iota(jnp.int32, (TOK, PEERS * 16), 1)
        pick = jnp.where(at == peer_of * 16 + position, 1.0, 0.0).astype(BF)
        gates = jnp.dot(
            pick,
            ret_in[:, CAP * SUB : BACK, :].reshape(PEERS * 16, LANES),
            preferred_element_type=F32,
        )
        ggrad_ref[...] = (gates[:, 0:1] / gate).astype(BF)
        out.wait()

    def drain():
        for c in range(CHUNKS):
            for h in range(2):
                at = remote_slots(c)
                pltpu.make_async_copy(
                    out_rows.at[h, at], in_rows.at[h, at], disp_send.at[h, c]
                ).wait()
                for kind in range(4):
                    gather_copy(c, h, kind).wait_send()
            for kind in range(6):
                scatter_copy(c, kind).wait_send()
            at = returned(c)
            pltpu.make_async_copy(ret_out.at[at], ret_in.at[at], ret_send.at[c]).wait()

    loads[0].wait()
    sort(0, 0)
    pl.semaphore_wait(barrier, PEERS - 1 + 2)
    dispatch(0, 0)
    loads[1].wait()
    for j in range(0, D, 1024):
        src[1, :, j : j + 1024] = (gate * src[1, :, j : j + 1024].astype(F32)).astype(BF)

    def sd(c, h):
        sort(c, h)
        dispatch(c, h)

    sd(0, 1)
    sd(1, 0)
    sd(1, 1)
    arrive(0, 0)
    arrive(0, 1)
    sd(2, 0)
    sd(2, 1)
    forward(0, 0)
    sd(3, 0)
    sd(3, 1)
    arrive(1, 0)
    forward(0, 1)
    compute(0, 0)
    arrive(1, 1)
    forward(1, 0)
    compute(0, 1)
    arrive(2, 0)
    forward(1, 1)
    compute(1, 0)
    pass_on(0)
    arrive(2, 1)
    forward(2, 0)
    compute(1, 1)
    send_home(0)
    arrive(3, 0)
    forward(2, 1)
    compute(2, 0)
    pass_on(1)
    arrive(3, 1)
    forward(3, 0)
    compute(2, 1)
    send_home(1)
    forward(3, 1)
    compute(3, 0)
    pass_on(2)
    compute(3, 1)
    send_home(2)
    come_home(0)
    come_home(1)
    pass_on(3)
    come_home(2)
    send_home(3)
    come_home(3)
    finish()
    drain()


def local(tokens, cotangent, expert_ids, gate_values, gate_weight, up_weight, down_weight):
    vmem = pl.BlockSpec(memory_space=pltpu.VMEM)
    hbm = pl.BlockSpec(memory_space=pl.ANY)
    dma = pltpu.SemaphoreType.DMA
    return pl.pallas_call(
        kernel,
        out_shape=(
            jax.ShapeDtypeStruct((TOK, D), BF),
            jax.ShapeDtypeStruct((TOK, 1), BF),
        ),
        in_specs=[hbm, hbm, vmem, vmem, hbm, hbm, hbm],
        out_specs=(hbm, vmem),
        scratch_shapes=[
            pltpu.VMEM((2, TOK, D), BF),
            pltpu.VMEM((3, HID, D), BF),
            pltpu.VMEM((2, SLOTS, SUB, LANES), BF),
            pltpu.VMEM((2, SLOTS, SUB, LANES), BF),
            pltpu.VMEM((2, CHUNKS, MANY, D), BF),
            pltpu.VMEM((2, MANY, HID), F32),
            pltpu.VMEM((CHUNKS, MANY, WIDE), BF),
            pltpu.VMEM((CHUNKS, ROWS, WIDE), BF),
            pltpu.VMEM((CHUNKS, 2, ROWS, WIDE), BF),
            pltpu.VMEM((PEERS, BACK, LANES), BF),
            pltpu.VMEM((PEERS, BACK, LANES), BF),
            pltpu.VMEM((SLOTS, D), BF),
            pltpu.VMEM((TOK, D), BF),
            dma((2,)),
            dma((3,)),
            dma((2, CHUNKS)),
            dma((2, CHUNKS)),
            dma((2, CHUNKS, 4)),
            dma((2, CHUNKS, 4)),
            dma((CHUNKS, 6)),
            dma((CHUNKS, 6)),
            dma((CHUNKS,)),
            dma((CHUNKS,)),
            dma,
        ],
        compiler_params=pltpu.CompilerParams(
            collective_id=0, has_side_effects=True, vmem_limit_bytes=60 * 2**20
        ),
    )(tokens, cotangent, expert_ids, gate_values, gate_weight, up_weight, down_weight)


def solution(mesh):
    rows = P(("expert", "tensor"), None)
    blocks = P(("expert", "tensor"), None, None)
    return jax.shard_map(
        local,
        mesh=mesh,
        in_specs=(rows, rows, rows, rows, blocks, blocks, blocks),
        out_specs=(rows, rows),
        check_vma=False,
    )
```

time: 642 us -> 212 us (0.33); the launches traced: 631 us -> 212 us
  waiting for transfers between devices: 333 us -> 0 us
  Pallas kernels: 0 us -> 205 us
  local copies, waits for them, and re-layouts: 173 us -> 6.41 us
  starting transfers between devices: 53 us -> 0 us
  matrix products: 38.5 us -> 0 us
  blocking collectives: 17.1 us -> 0 us
  other arithmetic: 15.2 us -> 0 us
    all_to_all x9 -> x0, waiting for transfers between devices: 333 us -> none  [the longest x1 93.7 us: local(): lax.all_to_all(copy_rows, 'tensor', split_axis=0, concat_axis=0, tiled=True)]
    pallas_call x0 -> x1, Pallas kernels: none -> 205 us  [local(): pl.pallas_call(kernel, out_shape=(jax.ShapeDtypeStruct((TOK, D), BF), jax...]
    reshape x12 -> x0, local copies, waits for them, and re-layouts: 73.9 us -> none  [the longest x2 24.1 us: local(): row_part = row_part.reshape(tensor_count, groups, capacity, model_width)]
    all_to_all x9 -> x0, starting transfers between devices: 53 us -> none  [the longest x1 6.98 us: local(): lax.all_to_all(copy_rows, 'tensor', split_axis=0, concat_axis=0, tiled=True)]
    dot_general x6 -> x0, matrix products: 38.5 us -> none  [the longest x1 8.48 us: expert_block(): jnp.einsum('mf,fd->md', d_pre_up, w_up, preferred_element_type=jnp.float32)]
    all_to_all x7 -> x0, local copies, waits for them, and re-layouts: 34.5 us -> none  [the longest x1 11.5 us: local(): lax.all_to_all(copy_rows, 'tensor', split_axis=0, concat_axis=0, tiled=True)]
    convert_element_type x4 -> x0, local copies, waits for them, and re-layouts: 26.3 us -> none  [the longest x2 25.3 us: expert_block(): (rows_gate.astype(jnp.float32)[:, None] * rows_cot.astype(jnp.float32)).a...]
    gather x5 -> x0, local copies, waits for them, and re-layouts: 19.3 us -> none  [the longest x1 5.65 us: local(): cot_pad[token_row].reshape(per_group, groups, capacity, model_width)]
  transfers between devices with their start and end apart: 9 -> 0, of which waited for: 7 -> 0; matrix products, arithmetic and copies ran while one was open for 26% -> 0% of each run, Pallas kernels for 0% -> 0%
where the time goes in v1:
time: 212 us
  Pallas kernels  205 us (97%)
  local copies, waits for them, and re-layouts  6.41 us (3%)
    pallas_call x1, Pallas kernels, local(): pl.pallas_call(kernel, out_shape=(jax.ShapeDtypeStruct((TOK, D), BF), jax...  205 us
    unnamed x3, local copies, waits for them, and re-layouts  5.06 us

profile of v1, /device:TPU:1, one launch (start us, length us, event | category | flops | bytes accessed | tf_op | source)
XLA Modules:
  0.0 211.6 jit_solution(5494129715281179637)
XLA Ops:
  0.6 1.4 copy.10.gate_ref
  2.0 1.4 copy.9.ids_ref
  3.4 204.6 %shard_map.86 = (bf16[128,4096]{1,0:T(8,128)(2,1)}, bf16[128,1]{1,0:T(8,128)(2,1)}) custom-call(bf16[128,4096]{1,0:T(8,128)(2,1)} %tok_hbm.1, bf16[128,4096]{1,0:T(8,128)(2,1)} %cot_hbm.1, s32[128,1]{1,0:T(8,128)} %copy.9.ids_ref, bf16[128,1]{1,0:T(8,128)(2,1)} %copy.10.gate_ref, bf16[1,384,4096]{2,1,0:T(8,128)(2,1)} %wg_hbm.1, ...), custom_call_target="tpu_custom_call" | custom-call | tf_op jit(solution)/shard_map/pallas_call | solution.py:427
  208.0 1.4 copy.11
  209.4 2.3 %copy.13 = bf16[128,4096]{1,0:T(8,128)(2,1)} copy(bf16[128,4096]{1,0:T(8,128)(2,1)} %get-tuple-element.6) | data formatting | bytes 2097152

commit v2 on v1

v2 whole, which is shorter than its diff:
```python
import functools

import jax
import jax.numpy as jnp
from jax import lax
from jax.experimental import pallas as pl
from jax.experimental.pallas import tpu as pltpu
from jax.sharding import PartitionSpec as P

MESH = pl.DeviceIdType.MESH
BF = jnp.bfloat16
F32 = jnp.float32

D = 4096
HID = 384
TOK = 128
CAP = 3
NZ, NY, NC, NX = 8, 4, 2, 4
PEERS = NZ * NY * NC
SLOTS = PEERS * CAP
CHUNKS = 4
PER = PEERS // CHUNKS
ROWS = PER * CAP
MANY = ROWS * NX
LANES = 128
SUB = D // LANES
WIDE = D + LANES
HALF = D // 2
KTILE = 1024
NTILE = 512
STEP = 2048
UNSORT = 2048
PIECE = CAP * SUB // 2
BACK = CAP * SUB + 16
ZORD = (0, 1, 4, 7, 3, 5, 2, 6)
NT = (((1,), (1,)), ((), ()))


def kernel(
    tok_hbm,
    cot_hbm,
    ids_ref,
    gate_ref,
    wg_hbm,
    wu_hbm,
    wd_hbm,
    home_hbm,
    ggrad_ref,
    slot_ref,
    src,
    wts,
    out_rows,
    in_rows,
    xrows,
    pre,
    grads,
    part,
    relay,
    full,
    ret_out,
    ret_in,
    home,
    load_sem,
    w_sem,
    disp_send,
    disp_recv,
    ag_send,
    ag_recv,
    rs_send,
    rs_recv,
    ret_send,
    ret_recv,
    out_sem,
):
    expert = lax.axis_index("expert")
    tensor = lax.axis_index("tensor")
    mz, mc = expert // NC, expert % NC
    my, mx = tensor // NX, tensor % NX

    def device(z, c, y, x):
        return (z * NC + c, y * NX + x)

    def each_peer(first, last, sign, act):
        def plane(q, carry):
            kz = jnp.int32(ZORD[0])
            for i in range(1, NZ):
                kz = jnp.where(q == i, ZORD[i], kz)
            z = lax.rem(mz + sign * kz + NZ, NZ)
            for j in range(NY * NC):
                y = lax.rem(my + sign * (j // NC) + NY, NY)
                to = device(z, lax.rem(mc + j % NC, NC), y, mx)
                k = q * NY * NC + j
                if j == 0:
                    pl.when(q > 0)(functools.partial(act, k, to))
                else:
                    act(k, to)
            return carry

        lax.fori_loop(first, last, plane, 0)

    right = device(mz, mc, my, lax.rem(mx + 1, NX))
    left = device(mz, mc, my, lax.rem(mx + NX - 1, NX))

    loads = [
        pltpu.make_async_copy(tok_hbm, src.at[0], load_sem.at[0]),
        pltpu.make_async_copy(cot_hbm, src.at[1], load_sem.at[1]),
    ]
    weight_loads = [
        pltpu.make_async_copy(w.at[0], wts.at[i], w_sem.at[i])
        for i, w in enumerate((wg_hbm, wu_hbm, wd_hbm))
    ]
    for copy in loads + weight_loads:
        copy.start()

    barrier = pltpu.get_barrier_semaphore()

    def greet(k, to):
        pl.semaphore_signal(barrier, inc=1, device_id=to, device_id_type=MESH)

    each_peer(0, NZ, 1, greet)
    for neighbour in (left, right):
        pl.semaphore_signal(barrier, inc=1, device_id=neighbour, device_id_type=MESH)

    t0 = lax.broadcasted_iota(jnp.int32, (TOK, TOK), 0)
    t1 = lax.broadcasted_iota(jnp.int32, (TOK, TOK), 1)
    ids_row = ids_ref[...]
    ids = jnp.sum(jnp.where(t0 == t1, ids_row, 0), axis=1, keepdims=True)
    earlier = jnp.where((ids == ids_row) & (t1 < t0), 1, 0)
    position = jnp.sum(earlier, axis=1, keepdims=True)
    kz = ((ids >> 3) - mz) & (NZ - 1)
    kc = ((ids >> 2) - mc) & (NC - 1)
    ky = (ids - my) & (NY - 1)
    q_of = jnp.zeros_like(kz)
    for q in range(NZ):
        q_of = jnp.where(kz == ZORD[q], q, q_of)
    peer_of = (q_of * NY + ky) * NC + kc
    slot = peer_of * CAP + position
    slot_row = jnp.sum(jnp.where(t0 == t1, slot, 0), axis=0, keepdims=True)
    gate = jnp.sum(
        jnp.where(t0 == t1, gate_ref[...].astype(F32), 0.0), axis=1, keepdims=True
    )

    def columns(j):
        return pl.ds(pl.multiple_of(j * STEP, STEP), STEP)

    def tiles(j):
        return pl.ds(pl.multiple_of(j * (STEP // LANES), STEP // LANES), STEP // LANES)

    def sort(c, h):
        at = lax.broadcasted_iota(jnp.int32, (ROWS, TOK), 0) + c * ROWS
        pick = jnp.where(at == slot_row, 1.0, 0.0).astype(BF)

        def tile(j, carry):
            rows = jnp.dot(pick, src[h, :, columns(j)], preferred_element_type=F32)
            out_rows[h, pl.ds(c * ROWS, ROWS), tiles(j), :] = pltpu.einshape(
                "a(bc)->abc", rows.astype(BF), c=LANES
            )
            return carry

        lax.fori_loop(0, D // STEP, tile, 0)

    def dispatch(c, h):

        def send(k, to):
            at = pl.ds(k * CAP, CAP)
            pltpu.make_async_remote_copy(
                src_ref=out_rows.at[h, at],
                dst_ref=in_rows.at[h, at],
                send_sem=disp_send.at[h, c],
                recv_sem=disp_recv.at[h, c],
                device_id=to,
                device_id_type=MESH,
            ).start()

        each_peer(c * NZ // CHUNKS, (c + 1) * NZ // CHUNKS, 1, send)

    def await_dispatch(c, h, sem):
        def wait(at):
            pltpu.make_async_copy(
                out_rows.at[h, at], in_rows.at[h, at], sem.at[h, c]
            ).wait()

        @pl.when(c == 0)
        def _():
            wait(pl.ds(CAP, ROWS - CAP))

        @pl.when(c > 0)
        def _():
            wait(pl.ds(c * ROWS, ROWS))

    def gather_copy(c, h, kind):
        x = xrows.at[h, c]
        own, from_left, far, from_right = (pl.ds(i * ROWS, ROWS) for i in range(4))
        a, b = pl.ds(0, HALF), pl.ds(HALF, HALF)
        ref_pair, to = (
            ((x.at[own], x.at[from_left]), right),
            ((x.at[own], x.at[from_right]), left),
            ((x.at[from_left, a], x.at[far, a]), right),
            ((x.at[from_right, b], x.at[far, b]), left),
        )[kind]
        return pltpu.make_async_remote_copy(
            src_ref=ref_pair[0],
            dst_ref=ref_pair[1],
            send_sem=ag_send.at[h, c, kind],
            recv_sem=ag_recv.at[h, c, kind],
            device_id=to,
            device_id_type=MESH,
        )

    def arrive(c, h):
        await_dispatch(c, h, disp_recv)

        @pl.when(c == 0)
        def _():
            in_rows[h, 0:CAP] = out_rows[h, 0:CAP]

        def tile(j, carry):
            xrows[h, c, 0:ROWS, columns(j)] = pltpu.einshape(
                "abc->a(bc)", in_rows[h, pl.ds(c * ROWS, ROWS), tiles(j), :]
            )
            return carry

        lax.fori_loop(0, D // STEP, tile, 0)
        gather_copy(c, h, 0).start()
        gather_copy(c, h, 1).start()

    def forward(c, h):
        gather_copy(c, h, 0).wait_recv()
        gather_copy(c, h, 2).start()
        gather_copy(c, h, 1).wait_recv()
        gather_copy(c, h, 3).start()

    def project(c, h, w):
        pre[w] = jnp.zeros((MANY, HID), F32)

        def add(k, carry):
            at = pl.ds(pl.multiple_of(k * KTILE, KTILE), KTILE)
            pre[w] += lax.dot_general(
                xrows[h, c, :, at], wts[w, :, at], NT, preferred_element_type=F32
            )
            return carry

        lax.fori_loop(0, D // KTILE, add, 0)

    def compute(c, h):
        gather_copy(c, h, 2).wait_recv()
        gather_copy(c, h, 3).wait_recv()
        if h == 0:

            @pl.when(c == 0)
            def _():
                weight_loads[0].wait()
                weight_loads[1].wait()

            project(c, 0, 0)
            project(c, 0, 1)
            return

        @pl.when(c == 0)
        def _():
            weight_loads[2].wait()

        project(c, 1, 2)
        pre_gate, pre_up, d_hidden = pre[0], pre[1], pre[2]
        sigmoid_gate = jax.nn.sigmoid(pre_gate)
        swish_gate = pre_gate * sigmoid_gate
        hidden = (swish_gate * pre_up).astype(BF).astype(F32)
        gate_part = jnp.sum(hidden * d_hidden, axis=1, keepdims=True)
        part[c, :, D:WIDE] = jnp.broadcast_to(gate_part, (MANY, LANES)).astype(BF)
        d_gate = (
            d_hidden * pre_up * sigmoid_gate * (1.0 + pre_gate * (1.0 - sigmoid_gate))
        ).astype(BF)
        d_up = (d_hidden * swish_gate).astype(BF)
        grads[0] = d_gate
        grads[1] = d_up

        def unproject(k, carry):
            at = pl.ds(pl.multiple_of(k * NTILE, NTILE), NTILE)
            part[c, :, at] = (
                jnp.dot(grads[0], wts[0, :, at], preferred_element_type=F32)
                + jnp.dot(grads[1], wts[1, :, at], preferred_element_type=F32)
            ).astype(BF)
            return carry

        for t in range(2):
            lax.fori_loop(
                t * HALF // NTILE, (t + 1) * HALF // NTILE, unproject, 0
            )
            for kind in range(4):
                scatter_copy(c, t, kind).start()

    def scatter_columns(t, side):
        start = t * HALF + side * HALF // 2
        return start, (WIDE if t == 1 and side == 1 else start + HALF // 2)

    def scatter_copy(c, t, kind):
        p = part.at[c]
        from_left_rows, far, from_right_rows = (pl.ds(i * ROWS, ROWS) for i in (1, 2, 3))
        a, b = (pl.ds(i, j - i) for i, j in (scatter_columns(t, 0), scatter_columns(t, 1)))
        ref_pair, to = (
            ((p.at[far, a], relay.at[c, :, a]), right),
            ((p.at[far, b], relay.at[c, :, b]), left),
            ((p.at[from_right_rows, b], full.at[c, 0, :, b]), right),
            ((p.at[from_left_rows, a], full.at[c, 1, :, a]), left),
            ((p.at[from_right_rows, a], full.at[c, 0, :, a]), right),
            ((p.at[from_left_rows, b], full.at[c, 1, :, b]), left),
        )[kind]
        return pltpu.make_async_remote_copy(
            src_ref=ref_pair[0],
            dst_ref=ref_pair[1],
            send_sem=rs_send.at[c, t, kind],
            recv_sem=rs_recv.at[c, t, kind],
            device_id=to,
            device_id_type=MESH,
        )

    def pass_on(c, t):
        for kind, rows in ((0, slice(3 * ROWS, 4 * ROWS)), (1, slice(ROWS, 2 * ROWS))):
            scatter_copy(c, t, kind).wait_recv()
            cols = slice(*scatter_columns(t, kind))
            part[c, rows, cols] = (
                part[c, rows, cols].astype(F32) + relay[c, :, cols].astype(F32)
            ).astype(BF)
            scatter_copy(c, t, kind + 4).start()

    def send_home(c, t):
        for kind in (2, 3, 4, 5):
            scatter_copy(c, t, kind).wait_recv()

        def total(at):
            return (
                part[c, 0:ROWS, at].astype(F32)
                + full[c, 0, :, at].astype(F32)
                + full[c, 1, :, at].astype(F32)
            ).astype(BF)

        rows = pltpu.einshape(
            "a(bc)->abc", total(slice(t * HALF, (t + 1) * HALF)), c=LANES
        )
        ret_out[pl.ds(c * PER, PER), t * PIECE : (t + 1) * PIECE, :] = rows.reshape(
            PER, PIECE, LANES
        )
        if t == 1:
            r0 = lax.broadcasted_iota(jnp.int32, (PER * 16, ROWS), 0)
            r1 = lax.broadcasted_iota(jnp.int32, (PER * 16, ROWS), 1)
            spread = jnp.where(
                (r1 == (r0 >> 4) * CAP + (r0 & 15)) & ((r0 & 15) < CAP), 1.0, 0.0
            ).astype(BF)
            gates = jnp.dot(spread, total(slice(D, WIDE)), preferred_element_type=F32)
            ret_out[pl.ds(c * PER, PER), CAP * SUB : BACK, :] = gates.astype(BF).reshape(
                PER, 16, LANES
            )

        def send(k, to):
            pltpu.make_async_remote_copy(
                src_ref=ret_out.at[k, returned(t)],
                dst_ref=ret_in.at[k, returned(t)],
                send_sem=ret_send.at[c, t],
                recv_sem=ret_recv.at[c, t],
                device_id=to,
                device_id_type=MESH,
            ).start()

        each_peer(c * NZ // CHUNKS, (c + 1) * NZ // CHUNKS, -1, send)

        @pl.when(c == 0)
        def _():
            ret_in[0, returned(t)] = ret_out[0, returned(t)]

    def returned(t):
        return pl.ds(0, PIECE) if t == 0 else pl.ds(PIECE, BACK - PIECE)

    def await_return(c, t, sem):
        def wait(at):
            pltpu.make_async_copy(
                ret_out.at[at, returned(t)], ret_in.at[at, returned(t)], sem.at[c, t]
            ).wait()

        @pl.when(c == 0)
        def _():
            wait(pl.ds(1, PER - 1))

        @pl.when(c > 0)
        def _():
            wait(pl.ds(c * PER, PER))

    def home_copy(c):
        at = pl.ds(c * ROWS, ROWS)
        return pltpu.make_async_copy(home.at[at], home_hbm.at[at], out_sem.at[c])

    def come_home(c):
        for t in range(2):
            await_return(c, t, ret_recv)
            rows = ret_in[pl.ds(c * PER, PER), t * PIECE : (t + 1) * PIECE, :]
            home[pl.ds(c * ROWS, ROWS), t * HALF : (t + 1) * HALF] = pltpu.einshape(
                "abc->a(bc)", rows.reshape(ROWS, SUB // 2, LANES)
            )
        home_copy(c).start()

    def finish():
        at = lax.broadcasted_iota(jnp.int32, (TOK, PEERS * 16), 1)
        pick = jnp.where(at == peer_of * 16 + position, 1.0, 0.0).astype(BF)
        gates = jnp.dot(
            pick,
            ret_in[:, CAP * SUB : BACK, :].reshape(PEERS * 16, LANES),
            preferred_element_type=F32,
        )
        ggrad = jnp.where(t0 == t1, gates / gate, 0.0)
        ggrad_ref[...] = jnp.sum(ggrad, axis=0, keepdims=True)
        slot_ref[...] = slot_row

    def drain():
        def ended(c, carry):
            for h in range(2):
                await_dispatch(c, h, disp_send)
                for kind in range(4):
                    gather_copy(c, h, kind).wait_send()
            for t in range(2):
                for kind in range(6):
                    scatter_copy(c, t, kind).wait_send()
                await_return(c, t, ret_send)
            home_copy(c).wait()
            return carry

        lax.fori_loop(0, CHUNKS, ended, 0)

    loads[0].wait()
    sort(0, 0)
    pl.semaphore_wait(barrier, PEERS - 1 + 2)
    dispatch(0, 0)
    loads[1].wait()
    for j in range(0, D, 1024):
        src[1, :, j : j + 1024] = (gate * src[1, :, j : j + 1024].astype(F32)).astype(BF)

    def sd(c, h):
        sort(c, h)
        dispatch(c, h)

    sd(0, 1)
    arrive(0, 0)
    lax.fori_loop(2, 4, lambda n, carry: sd(n // 2, n % 2) or carry, 0)
    arrive(0, 1)
    lax.fori_loop(4, 6, lambda n, carry: sd(n // 2, n % 2) or carry, 0)
    forward(0, 0)
    lax.fori_loop(6, 8, lambda n, carry: sd(n // 2, n % 2) or carry, 0)

    def step(c, carry):
        @pl.when(c < CHUNKS - 1)
        def _():
            arrive(c + 1, 0)

        forward(c, 1)
        compute(c, 0)

        @pl.when(c > 0)
        def _():
            pass_on(c - 1, 0)
            pass_on(c - 1, 1)

        @pl.when(c < CHUNKS - 1)
        def _():
            arrive(c + 1, 1)
            forward(c + 1, 0)

        compute(c, 1)

        @pl.when(c > 0)
        def _():
            send_home(c - 1, 0)
            send_home(c - 1, 1)

        return carry

    lax.fori_loop(0, CHUNKS, step, 0)
    pass_on(CHUNKS - 1, 0)
    pass_on(CHUNKS - 1, 1)
    lax.fori_loop(0, 2, lambda c, carry: come_home(c) or carry, 0)
    send_home(CHUNKS - 1, 0)
    send_home(CHUNKS - 1, 1)
    lax.fori_loop(2, CHUNKS, lambda c, carry: come_home(c) or carry, 0)
    finish()
    drain()


def unsort(home_ref, gate_ref, slot_ref, dtok_ref, ggrad_ref):
    t0 = lax.broadcasted_iota(jnp.int32, (TOK, TOK), 0)
    t1 = lax.broadcasted_iota(jnp.int32, (TOK, TOK), 1)
    slot = jnp.sum(jnp.where(t0 == t1, slot_ref[...], 0), axis=1, keepdims=True)
    at = lax.broadcasted_iota(jnp.int32, (TOK, SLOTS), 1)
    pick = jnp.where(at == slot, 1.0, 0.0).astype(BF)
    dtok_ref[...] = jnp.dot(pick, home_ref[...], preferred_element_type=F32).astype(BF)
    ggrad_ref[...] = gate_ref[...].astype(BF)


def local(tokens, cotangent, expert_ids, gate_values, gate_weight, up_weight, down_weight):
    vmem = pl.BlockSpec(memory_space=pltpu.VMEM)
    hbm = pl.BlockSpec(memory_space=pl.ANY)
    dma = pltpu.SemaphoreType.DMA
    home, gate_grad, slot = pl.pallas_call(
        kernel,
        out_shape=(
            jax.ShapeDtypeStruct((SLOTS, D), BF),
            jax.ShapeDtypeStruct((1, TOK), F32),
            jax.ShapeDtypeStruct((1, TOK), jnp.int32),
        ),
        in_specs=[hbm, hbm, vmem, vmem, hbm, hbm, hbm],
        out_specs=(hbm, vmem, vmem),
        scratch_shapes=[
            pltpu.VMEM((2, TOK, D), BF),
            pltpu.VMEM((3, HID, D), BF),
            pltpu.VMEM((2, SLOTS, SUB, LANES), BF),
            pltpu.VMEM((2, SLOTS, SUB, LANES), BF),
            pltpu.VMEM((2, CHUNKS, MANY, D), BF),
            pltpu.VMEM((3, MANY, HID), F32),
            pltpu.VMEM((2, MANY, HID), BF),
            pltpu.VMEM((CHUNKS, MANY, WIDE), BF),
            pltpu.VMEM((CHUNKS, ROWS, WIDE), BF),
            pltpu.VMEM((CHUNKS, 2, ROWS, WIDE), BF),
            pltpu.VMEM((PEERS, BACK, LANES), BF),
            pltpu.VMEM((PEERS, BACK, LANES), BF),
            pltpu.VMEM((SLOTS, D), BF),
            dma((2,)),
            dma((3,)),
            dma((2, CHUNKS)),
            dma((2, CHUNKS)),
            dma((2, CHUNKS, 4)),
            dma((2, CHUNKS, 4)),
            dma((CHUNKS, 2, 6)),
            dma((CHUNKS, 2, 6)),
            dma((CHUNKS, 2)),
            dma((CHUNKS, 2)),
            dma((CHUNKS,)),
        ],
        compiler_params=pltpu.CompilerParams(
            collective_id=0, has_side_effects=True, vmem_limit_bytes=60 * 2**20
        ),
    )(
        tokens,
        cotangent,
        expert_ids.reshape(1, TOK),
        gate_values.reshape(1, TOK),
        gate_weight,
        up_weight,
        down_weight,
    )
    d_tokens, gate_grad = pl.pallas_call(
        unsort,
        grid=(D // UNSORT,),
        out_shape=(
            jax.ShapeDtypeStruct((TOK, D), BF),
            jax.ShapeDtypeStruct((1, TOK), BF),
        ),
        in_specs=[
            pl.BlockSpec((SLOTS, UNSORT), lambda j: (0, j)),
            pl.BlockSpec((1, TOK), lambda j: (0, 0)),
            pl.BlockSpec((1, TOK), lambda j: (0, 0)),
        ],
        out_specs=(
            pl.BlockSpec((TOK, UNSORT), lambda j: (0, j)),
            pl.BlockSpec((1, TOK), lambda j: (0, 0)),
        ),
    )(home, gate_grad, slot)
    return d_tokens, gate_grad.reshape(TOK, 1)


def solution(mesh):
    rows = P(("expert", "tensor"), None)
    blocks = P(("expert", "tensor"), None, None)
    return jax.shard_map(
        local,
        mesh=mesh,
        in_specs=(rows, rows, rows, rows, blocks, blocks, blocks),
        out_specs=(rows, rows),
        check_vma=False,
    )
```

time: 212 us -> 199 us (0.939)
  Pallas kernels: 205 us -> 198 us
  local copies, waits for them, and re-layouts: 6.41 us -> 0 us
    pallas_call x1 -> x2, Pallas kernels: 205 us -> 198 us  [the longest x1 196 us: local(): pl.pallas_call(kernel, out_shape=(jax.ShapeDtypeStruct((SLOTS, D), BF), j...]
    unnamed x3 -> x0, local copies, waits for them, and re-layouts: 5.06 us -> none
where the time goes in v2:
time: 199 us
  Pallas kernels  198 us (99%)
    pallas_call x1, Pallas kernels, local(): pl.pallas_call(kernel, out_shape=(jax.ShapeDtypeStruct((SLOTS, D), BF), j...  196 us

profile of v2, /device:TPU:1, one launch (start us, length us, event | category | flops | bytes accessed | tf_op | source)
XLA Modules:
  0.0 199.0 jit_solution(15492255615730171132)
XLA Ops:
  0.6 195.7 %shard_map.86 = (bf16[192,4096]{1,0:T(8,128)(2,1)}, f32[1,128]{1,0:T(1,128)}, s32[1,128]{1,0:T(1,128)}) custom-call(bf16[128,4096]{1,0:T(8,128)(2,1)} %tok_hbm.1, bf16[128,4096]{1,0:T(8,128)(2,1)} %cot_hbm.1, s32[1,128]{1,0:T(1,128)} %bitcast.3, bf16[1,128]{1,0:T(2,128)(2,1)} %bitcast.4, bf16[1,384,4096]{2,1,0:T(8,128)(2,1)} %wg_hbm.1, ...), custom_call_target="tpu_custom_call" | custom-call | tf_op jit(solution)/shard_map/pallas_call | solution.py:499
  196.3 2.7 %shard_map.87 = (bf16[128,4096]{1,0:T(8,128)(2,1)}, bf16[1,128]{1,0:T(2,128)(2,1)}) custom-call(bf16[192,4096]{1,0:T(8,128)(2,1)} %get-tuple-element.7.home_ref, f32[1,128]{1,0:T(1,128)} %get-tuple-element.8.gate_ref, s32[1,128]{1,0:T(1,128)} %get-tuple-element.9.slot_ref), custom_call_target="tpu_custom_call" | custom-call | tf_op jit(solution)/shard_map/pallas_call | solution.py:546

commit v3 on v2

--- a/solution.py
+++ b/solution.py
@@ -24,15 +24,22 @@
 MANY = ROWS * NX
 LANES = 128
 SUB = D // LANES
-WIDE = D + LANES
+WIDE = LANES + D
 HALF = D // 2
 KTILE = 1024
 NTILE = 512
+SPLIT = 2
+PIECES = 2 * SPLIT
+SPAN = D // SPLIT
+PSUB = SPAN // LANES
 STEP = 2048
 UNSORT = 2048
 PIECE = CAP * SUB // 2
-BACK = CAP * SUB + 16
-ZORD = (0, 1, 4, 7, 3, 5, 2, 6)
+BACK = 16 + CAP * SUB
+ORDER = (2, 14, 4, 12, 6, 7, 10, 11, 8, 9, 5, 13, 0, 3, 15, 1)
+GROUPS = NZ * NC
+SELF = ORDER.index(0)
+SELF_CHUNK = SELF * CHUNKS // GROUPS
 NT = (((1,), (1,)), ((), ()))
 
 
@@ -81,22 +88,22 @@
         return (z * NC + c, y * NX + x)
 
     def each_peer(first, last, sign, act):
-        def plane(q, carry):
-            kz = jnp.int32(ZORD[0])
-            for i in range(1, NZ):
-                kz = jnp.where(q == i, ZORD[i], kz)
-            z = lax.rem(mz + sign * kz + NZ, NZ)
-            for j in range(NY * NC):
-                y = lax.rem(my + sign * (j // NC) + NY, NY)
-                to = device(z, lax.rem(mc + j % NC, NC), y, mx)
-                k = q * NY * NC + j
-                if j == 0:
-                    pl.when(q > 0)(functools.partial(act, k, to))
+        def group(q, carry):
+            code = jnp.int32(ORDER[0])
+            for i in range(1, GROUPS):
+                code = jnp.where(q == i, ORDER[i], code)
+            z = lax.rem(mz + sign * (code // NC) + NZ, NZ)
+            core = lax.rem(mc + code % NC, NC)
+            for ky in range(NY):
+                to = device(z, core, lax.rem(my + sign * ky + NY, NY), mx)
+                k = q * NY + ky
+                if ky == 0:
+                    pl.when(q != SELF)(functools.partial(act, k, to))
                 else:
                     act(k, to)
             return carry
 
-        lax.fori_loop(first, last, plane, 0)
+        lax.fori_loop(first, last, group, 0)
 
     right = device(mz, mc, my, lax.rem(mx + 1, NX))
     left = device(mz, mc, my, lax.rem(mx + NX - 1, NX))
@@ -117,7 +124,7 @@
     def greet(k, to):
         pl.semaphore_signal(barrier, inc=1, device_id=to, device_id_type=MESH)
 
-    each_peer(0, NZ, 1, greet)
+    each_peer(0, GROUPS, 1, greet)
     for neighbour in (left, right):
         pl.semaphore_signal(barrier, inc=1, device_id=neighbour, device_id_type=MESH)
 
@@ -131,9 +138,9 @@
     kc = ((ids >> 2) - mc) & (NC - 1)
     ky = (ids - my) & (NY - 1)
     q_of = jnp.zeros_like(kz)
-    for q in range(NZ):
-        q_of = jnp.where(kz == ZORD[q], q, q_of)
-    peer_of = (q_of * NY + ky) * NC + kc
+    for q in range(GROUPS):
+        q_of = jnp.where(kz * NC + kc == ORDER[q], q, q_of)
+    peer_of = q_of * NY + ky
     slot = peer_of * CAP + position
     slot_row = jnp.sum(jnp.where(t0 == t1, slot, 0), axis=0, keepdims=True)
     gate = jnp.sum(
@@ -146,89 +153,89 @@
     def tiles(j):
         return pl.ds(pl.multiple_of(j * (STEP // LANES), STEP // LANES), STEP // LANES)
 
-    def sort(c, h):
+    def sort(c, n):
         at = lax.broadcasted_iota(jnp.int32, (ROWS, TOK), 0) + c * ROWS
         pick = jnp.where(at == slot_row, 1.0, 0.0).astype(BF)
-
-        def tile(j, carry):
-            rows = jnp.dot(pick, src[h, :, columns(j)], preferred_element_type=F32)
-            out_rows[h, pl.ds(c * ROWS, ROWS), tiles(j), :] = pltpu.einshape(
+        for j in range(SPAN // STEP):
+            cols = columns(n % SPLIT * (SPAN // STEP) + j)
+            rows = jnp.dot(pick, src[n // SPLIT, :, cols], preferred_element_type=F32)
+            out_rows[n, pl.ds(c * ROWS, ROWS), tiles(j), :] = pltpu.einshape(
                 "a(bc)->abc", rows.astype(BF), c=LANES
             )
-            return carry
-
-        lax.fori_loop(0, D // STEP, tile, 0)
-
-    def dispatch(c, h):
+
+    def dispatch(c, n):
 
         def send(k, to):
             at = pl.ds(k * CAP, CAP)
             pltpu.make_async_remote_copy(
-                src_ref=out_rows.at[h, at],
-                dst_ref=in_rows.at[h, at],
-                send_sem=disp_send.at[h, c],
-                recv_sem=disp_recv.at[h, c],
+                src_ref=out_rows.at[n, at],
+                dst_ref=in_rows.at[n, at],
+                send_sem=disp_send.at[n, c],
+                recv_sem=disp_recv.at[n, c],
                 device_id=to,
                 device_id_type=MESH,
             ).start()
 
-        each_peer(c * NZ // CHUNKS, (c + 1) * NZ // CHUNKS, 1, send)
-
-    def await_dispatch(c, h, sem):
+        each_peer(c * GROUPS // CHUNKS, (c + 1) * GROUPS // CHUNKS, 1, send)
+
+    def await_dispatch(c, n, sem):
         def wait(at):
             pltpu.make_async_copy(
-                out_rows.at[h, at], in_rows.at[h, at], sem.at[h, c]
+                out_rows.at[n, at], in_rows.at[n, at], sem.at[n, c]
             ).wait()
 
-        @pl.when(c == 0)
-        def _():
-            wait(pl.ds(CAP, ROWS - CAP))
-
-        @pl.when(c > 0)
+        @pl.when(c == SELF_CHUNK)
+        def _():
+            wait(pl.ds(SELF_CHUNK * ROWS + CAP, ROWS - CAP))
+
+        @pl.when(c != SELF_CHUNK)
         def _():
             wait(pl.ds(c * ROWS, ROWS))
 
-    def gather_copy(c, h, kind):
-        x = xrows.at[h, c]
+    def gather_copy(c, n, kind):
+        x = xrows.at[n // SPLIT, c]
+        start = n % SPLIT * SPAN
         own, from_left, far, from_right = (pl.ds(i * ROWS, ROWS) for i in range(4))
-        a, b = pl.ds(0, HALF), pl.ds(HALF, HALF)
+        whole = pl.ds(start, SPAN)
+        a, b = pl.ds(start, SPAN // 2), pl.ds(start + SPAN // 2, SPAN // 2)
         ref_pair, to = (
-            ((x.at[own], x.at[from_left]), right),
-            ((x.at[own], x.at[from_right]), left),
+            ((x.at[own, whole], x.at[from_left, whole]), right),
+            ((x.at[own, whole], x.at[from_right, whole]), left),
             ((x.at[from_left, a], x.at[far, a]), right),
             ((x.at[from_right, b], x.at[far, b]), left),
         )[kind]
         return pltpu.make_async_remote_copy(
             src_ref=ref_pair[0],
             dst_ref=ref_pair[1],
-            send_sem=ag_send.at[h, c, kind],
-            recv_sem=ag_recv.at[h, c, kind],
+            send_sem=ag_send.at[n, c, kind],
+            recv_sem=ag_recv.at[n, c, kind],
             device_id=to,
             device_id_type=MESH,
         )
 
     def arrive(c, h):
-        await_dispatch(c, h, disp_recv)
-
-        @pl.when(c == 0)
-        def _():
-            in_rows[h, 0:CAP] = out_rows[h, 0:CAP]
-
-        def tile(j, carry):
-            xrows[h, c, 0:ROWS, columns(j)] = pltpu.einshape(
-                "abc->a(bc)", in_rows[h, pl.ds(c * ROWS, ROWS), tiles(j), :]
-            )
-            return carry
-
-        lax.fori_loop(0, D // STEP, tile, 0)
-        gather_copy(c, h, 0).start()
-        gather_copy(c, h, 1).start()
+        for n in range(h * SPLIT, (h + 1) * SPLIT):
+            await_dispatch(c, n, disp_recv)
+
+            @pl.when(c == SELF_CHUNK)
+            def _(n=n):
+                at = slice(SELF_CHUNK * ROWS, SELF_CHUNK * ROWS + CAP)
+                in_rows[n, at] = out_rows[n, at]
+
+            for j in range(SPAN // STEP):
+                cols = columns(n % SPLIT * (SPAN // STEP) + j)
+                xrows[h, c, 0:ROWS, cols] = pltpu.einshape(
+                    "abc->a(bc)", in_rows[n, pl.ds(c * ROWS, ROWS), tiles(j), :]
+                )
+            gather_copy(c, n, 0).start()
+            gather_copy(c, n, 1).start()
 
     def forward(c, h):
-        gather_copy(c, h, 0).wait_recv()
-        gather_copy(c, h, 2).start()
-        gather_copy(c, h, 1).wait_recv()
-        gather_copy(c, h, 3).start()
+        for n in range(h * SPLIT, (h + 1) * SPLIT):
+            gather_copy(c, n, 0).wait_recv()
+            gather_copy(c, n, 2).start()
+            gather_copy(c, n, 1).wait_recv()
+            gather_copy(c, n, 3).start()
 
     def project(c, h, w):
         pre[w] = jnp.zeros((MANY, HID), F32)
@@ -243,8 +250,9 @@
         lax.fori_loop(0, D // KTILE, add, 0)
 
     def compute(c, h):
-        gather_copy(c, h, 2).wait_recv()
-        gather_copy(c, h, 3).wait_recv()
+        for n in range(h * SPLIT, (h + 1) * SPLIT):
+            gather_copy(c, n, 2).wait_recv()
+            gather_copy(c, n, 3).wait_recv()
         if h == 0:
 
             @pl.when(c == 0)
@@ -266,7 +274,7 @@
         swish_gate = pre_gate * sigmoid_gate
         hidden = (swish_gate * pre_up).astype(BF).astype(F32)
         gate_part = jnp.sum(hidden * d_hidden, axis=1, keepdims=True)
-        part[c, :, D:WIDE] = jnp.broadcast_to(gate_part, (MANY, LANES)).astype(BF)
+        part[c, :, 0:LANES] = jnp.broadcast_to(gate_part, (MANY, LANES)).astype(BF)
         d_gate = (
             d_hidden * pre_up * sigmoid_gate * (1.0 + pre_gate * (1.0 - sigmoid_gate))
         ).astype(BF)
@@ -276,7 +284,8 @@
 
         def unproject(k, carry):
             at = pl.ds(pl.multiple_of(k * NTILE, NTILE), NTILE)
-            part[c, :, at] = (
+            to = pl.ds(pl.multiple_of(LANES + k * NTILE, LANES), NTILE)
+            part[c, :, to] = (
                 jnp.dot(grads[0], wts[0, :, at], preferred_element_type=F32)
                 + jnp.dot(grads[1], wts[1, :, at], preferred_element_type=F32)
             ).astype(BF)
@@ -290,8 +299,8 @@
                 scatter_copy(c, t, kind).start()
 
     def scatter_columns(t, side):
-        start = t * HALF + side * HALF // 2
-        return start, (WIDE if t == 1 and side == 1 else start + HALF // 2)
+        start = LANES + t * HALF + side * HALF // 2
+        return (0 if t == 0 and side == 0 else start), start + HALF // 2
 
     def scatter_copy(c, t, kind):
         p = part.at[c]
@@ -335,19 +344,19 @@
             ).astype(BF)
 
         rows = pltpu.einshape(
-            "a(bc)->abc", total(slice(t * HALF, (t + 1) * HALF)), c=LANES
+            "a(bc)->abc", total(slice(LANES + t * HALF, LANES + (t + 1) * HALF)), c=LANES
         )
-        ret_out[pl.ds(c * PER, PER), t * PIECE : (t + 1) * PIECE, :] = rows.reshape(
-            PER, PIECE, LANES
+        ret_out[pl.ds(c * PER, PER), 16 + t * PIECE : 16 + (t + 1) * PIECE, :] = (
+            rows.reshape(PER, PIECE, LANES)
         )
-        if t == 1:
+        if t == 0:
             r0 = lax.broadcasted_iota(jnp.int32, (PER * 16, ROWS), 0)
             r1 = lax.broadcasted_iota(jnp.int32, (PER * 16, ROWS), 1)
             spread = jnp.where(
                 (r1 == (r0 >> 4) * CAP + (r0 & 15)) & ((r0 & 15) < CAP), 1.0, 0.0
             ).astype(BF)
-            gates = jnp.dot(spread, total(slice(D, WIDE)), preferred_element_type=F32)
-            ret_out[pl.ds(c * PER, PER), CAP * SUB : BACK, :] = gates.astype(BF).reshape(
+            gates = jnp.dot(spread, total(slice(0, LANES)), preferred_element_type=F32)
+            ret_out[pl.ds(c * PER, PER), 0:16, :] = gates.astype(BF).reshape(
                 PER, 16, LANES
             )
 
@@ -361,14 +370,14 @@
                 device_id_type=MESH,
             ).start()
 
-        each_peer(c * NZ // CHUNKS, (c + 1) * NZ // CHUNKS, -1, send)
-
-        @pl.when(c == 0)
-        def _():
-            ret_in[0, returned(t)] = ret_out[0, returned(t)]
+        each_peer(c * GROUPS // CHUNKS, (c + 1) * GROUPS // CHUNKS, -1, send)
+
+        @pl.when(c == SELF_CHUNK)
+        def _():
+            ret_in[SELF_CHUNK * PER, returned(t)] = ret_out[SELF_CHUNK * PER, returned(t)]
 
     def returned(t):
-        return pl.ds(0, PIECE) if t == 0 else pl.ds(PIECE, BACK - PIECE)
+        return pl.ds(0, 16 + PIECE) if t == 0 else pl.ds(16 + PIECE, PIECE)
 
     def await_return(c, t, sem):
         def wait(at):
@@ -376,11 +385,11 @@
                 ret_out.at[at, returned(t)], ret_in.at[at, returned(t)], sem.at[c, t]
             ).wait()
 
-        @pl.when(c == 0)
-        def _():
-            wait(pl.ds(1, PER - 1))
-
-        @pl.when(c > 0)
+        @pl.when(c == SELF_CHUNK)
+        def _():
+            wait(pl.ds(SELF_CHUNK * PER + 1, PER - 1))
+
+        @pl.when(c != SELF_CHUNK)
         def _():
             wait(pl.ds(c * PER, PER))
 
@@ -391,7 +400,7 @@
     def come_home(c):
         for t in range(2):
             await_return(c, t, ret_recv)
-            rows = ret_in[pl.ds(c * PER, PER), t * PIECE : (t + 1) * PIECE, :]
+            rows = ret_in[pl.ds(c * PER, PER), 16 + t * PIECE : 16 + (t + 1) * PIECE, :]
             home[pl.ds(c * ROWS, ROWS), t * HALF : (t + 1) * HALF] = pltpu.einshape(
                 "abc->a(bc)", rows.reshape(ROWS, SUB // 2, LANES)
             )
@@ -402,7 +411,7 @@
         pick = jnp.where(at == peer_of * 16 + position, 1.0, 0.0).astype(BF)
         gates = jnp.dot(
             pick,
-            ret_in[:, CAP * SUB : BACK, :].reshape(PEERS * 16, LANES),
+            ret_in[:, 0:16, :].reshape(PEERS * 16, LANES),
             preferred_element_type=F32,
         )
         ggrad = jnp.where(t0 == t1, gates / gate, 0.0)
@@ -411,10 +420,10 @@
 
     def drain():
         def ended(c, carry):
-            for h in range(2):
-                await_dispatch(c, h, disp_send)
+            for n in range(PIECES):
+                await_dispatch(c, n, disp_send)
                 for kind in range(4):
-                    gather_copy(c, h, kind).wait_send()
+                    gather_copy(c, n, kind).wait_send()
             for t in range(2):
                 for kind in range(6):
                     scatter_copy(c, t, kind).wait_send()
@@ -424,25 +433,34 @@
 
         lax.fori_loop(0, CHUNKS, ended, 0)
 
+    def sd(c, h):
+        def piece(n, carry):
+            sort(c, n)
+            dispatch(c, n)
+            return carry
+
+        lax.fori_loop(h * SPLIT, (h + 1) * SPLIT, piece, 0)
+
     loads[0].wait()
     sort(0, 0)
     pl.semaphore_wait(barrier, PEERS - 1 + 2)
     dispatch(0, 0)
+    for n in range(1, SPLIT):
+        sort(0, n)
+        dispatch(0, n)
     loads[1].wait()
     for j in range(0, D, 1024):
         src[1, :, j : j + 1024] = (gate * src[1, :, j : j + 1024].astype(F32)).astype(BF)
-
-    def sd(c, h):
-        sort(c, h)
-        dispatch(c, h)
-
     sd(0, 1)
     arrive(0, 0)
-    lax.fori_loop(2, 4, lambda n, carry: sd(n // 2, n % 2) or carry, 0)
+    sd(1, 0)
+    sd(1, 1)
     arrive(0, 1)
-    lax.fori_loop(4, 6, lambda n, carry: sd(n // 2, n % 2) or carry, 0)
+    sd(2, 0)
+    sd(2, 1)
     forward(0, 0)
-    lax.fori_loop(6, 8, lambda n, carry: sd(n // 2, n % 2) or carry, 0)
+    sd(3, 0)
+    sd(3, 1)
 
     def step(c, carry):
         @pl.when(c < CHUNKS - 1)
@@ -508,8 +526,8 @@
         scratch_shapes=[
             pltpu.VMEM((2, TOK, D), BF),
             pltpu.VMEM((3, HID, D), BF),
-            pltpu.VMEM((2, SLOTS, SUB, LANES), BF),
-            pltpu.VMEM((2, SLOTS, SUB, LANES), BF),
+            pltpu.VMEM((PIECES, SLOTS, PSUB, LANES), BF),
+            pltpu.VMEM((PIECES, SLOTS, PSUB, LANES), BF),
             pltpu.VMEM((2, CHUNKS, MANY, D), BF),
             pltpu.VMEM((3, MANY, HID), F32),
             pltpu.VMEM((2, MANY, HID), BF),
@@ -521,10 +539,10 @@
             pltpu.VMEM((SLOTS, D), BF),
             dma((2,)),
             dma((3,)),
-            dma((2, CHUNKS)),
-            dma((2, CHUNKS)),
-            dma((2, CHUNKS, 4)),
-            dma((2, CHUNKS, 4)),
+            dma((PIECES, CHUNKS)),
+            dma((PIECES, CHUNKS)),
+            dma((PIECES, CHUNKS, 4)),
+            dma((PIECES, CHUNKS, 4)),
             dma((CHUNKS, 2, 6)),
             dma((CHUNKS, 2, 6)),
             dma((CHUNKS, 2)),

time: 199 us -> 191 us (0.960)
  Pallas kernels: 198 us -> 190 us
    pallas_call x1, Pallas kernels: 196 us -> 188 us  [local(): pl.pallas_call(kernel, out_shape=(jax.ShapeDtypeStruct((SLOTS, D), BF), j...]
where the time goes in v3:
time: 191 us
  Pallas kernels  190 us (99%)
    pallas_call x1, Pallas kernels, local(): pl.pallas_call(kernel, out_shape=(jax.ShapeDtypeStruct((SLOTS, D), BF), j...  188 us

profile of v3, /device:TPU:1, one launch (start us, length us, event | category | flops | bytes accessed | tf_op | source)
XLA Modules:
  0.0 191.1 jit_solution(11108998293974421719)
XLA Ops:
  0.6 187.8 %shard_map.86 = (bf16[192,4096]{1,0:T(8,128)(2,1)}, f32[1,128]{1,0:T(1,128)}, s32[1,128]{1,0:T(1,128)}) custom-call(bf16[128,4096]{1,0:T(8,128)(2,1)} %tok_hbm.1, bf16[128,4096]{1,0:T(8,128)(2,1)} %cot_hbm.1, s32[1,128]{1,0:T(1,128)} %bitcast.3, bf16[1,128]{1,0:T(2,128)(2,1)} %bitcast.4, bf16[1,384,4096]{2,1,0:T(8,128)(2,1)} %wg_hbm.1, ...), custom_call_target="tpu_custom_call" | custom-call | tf_op jit(solution)/shard_map/pallas_call | solution.py:517
  188.4 2.7 %shard_map.87 = (bf16[128,4096]{1,0:T(8,128)(2,1)}, bf16[1,128]{1,0:T(2,128)(2,1)}) custom-call(bf16[192,4096]{1,0:T(8,128)(2,1)} %get-tuple-element.7.home_ref, f32[1,128]{1,0:T(1,128)} %get-tuple-element.8.gate_ref, s32[1,128]{1,0:T(1,128)} %get-tuple-element.9.slot_ref), custom_call_target="tpu_custom_call" | custom-call | tf_op jit(solution)/shard_map/pallas_call | solution.py:564

commit v4 on v3

--- a/solution.py
+++ b/solution.py
@@ -36,7 +36,7 @@
 UNSORT = 2048
 PIECE = CAP * SUB // 2
 BACK = 16 + CAP * SUB
-ORDER = (2, 14, 4, 12, 6, 7, 10, 11, 8, 9, 5, 13, 0, 3, 15, 1)
+ORDER = (2, 14, 4, 12, 6, 10, 7, 11, 8, 9, 3, 15, 0, 5, 13, 1)
 GROUPS = NZ * NC
 SELF = ORDER.index(0)
 SELF_CHUNK = SELF * CHUNKS // GROUPS
@@ -237,22 +237,25 @@
             gather_copy(c, n, 1).wait_recv()
             gather_copy(c, n, 3).start()
 
-    def project(c, h, w):
-        pre[w] = jnp.zeros((MANY, HID), F32)
+    def project(c, h, ws):
+        for w in ws:
+            pre[w] = jnp.zeros((MANY, HID), F32)
 
         def add(k, carry):
             at = pl.ds(pl.multiple_of(k * KTILE, KTILE), KTILE)
-            pre[w] += lax.dot_general(
-                xrows[h, c, :, at], wts[w, :, at], NT, preferred_element_type=F32
-            )
+            for w in ws:
+                pre[w] += lax.dot_general(
+                    xrows[h, c, :, at], wts[w, :, at], NT, preferred_element_type=F32
+                )
             return carry
 
-        lax.fori_loop(0, D // KTILE, add, 0)
-
-    def compute(c, h):
-        for n in range(h * SPLIT, (h + 1) * SPLIT):
+        for i in range(SPLIT):
+            n = h * SPLIT + i
             gather_copy(c, n, 2).wait_recv()
             gather_copy(c, n, 3).wait_recv()
+            lax.fori_loop(i * SPAN // KTILE, (i + 1) * SPAN // KTILE, add, 0)
+
+    def compute(c, h):
         if h == 0:
 
             @pl.when(c == 0)
@@ -260,15 +263,14 @@
                 weight_loads[0].wait()
                 weight_loads[1].wait()
 
-            project(c, 0, 0)
-            project(c, 0, 1)
+            project(c, 0, (0, 1))
             return
 
         @pl.when(c == 0)
         def _():
             weight_loads[2].wait()
 
-        project(c, 1, 2)
+        project(c, 1, (2,))
         pre_gate, pre_up, d_hidden = pre[0], pre[1], pre[2]
         sigmoid_gate = jax.nn.sigmoid(pre_gate)
         swish_gate = pre_gate * sigmoid_gate

time: 191 us -> 190 us (level)
  no operation moved by 1% of the time
where the time goes in v4:
time: 190 us; the launch traced here: 189 us
  Pallas kernels  189 us (99%)
    pallas_call x1, Pallas kernels, local(): pl.pallas_call(kernel, out_shape=(jax.ShapeDtypeStruct((SLOTS, D), BF), j...  186 us

profile of v4, /device:TPU:1, one launch (start us, length us, event | category | flops | bytes accessed | tf_op | source)
XLA Modules:
  0.0 189.5 jit_solution(3379079217664339199)
XLA Ops:
  0.6 186.2 %shard_map.86 = (bf16[192,4096]{1,0:T(8,128)(2,1)}, f32[1,128]{1,0:T(1,128)}, s32[1,128]{1,0:T(1,128)}) custom-call(bf16[128,4096]{1,0:T(8,128)(2,1)} %tok_hbm.1, bf16[128,4096]{1,0:T(8,128)(2,1)} %cot_hbm.1, s32[1,128]{1,0:T(1,128)} %bitcast.3, bf16[1,128]{1,0:T(2,128)(2,1)} %bitcast.4, bf16[1,384,4096]{2,1,0:T(8,128)(2,1)} %wg_hbm.1, ...), custom_call_target="tpu_custom_call" | custom-call | tf_op jit(solution)/shard_map/pallas_call | solution.py:519
  186.8 2.7 %shard_map.87 = (bf16[128,4096]{1,0:T(8,128)(2,1)}, bf16[1,128]{1,0:T(2,128)(2,1)}) custom-call(bf16[192,4096]{1,0:T(8,128)(2,1)} %get-tuple-element.7.home_ref, f32[1,128]{1,0:T(1,128)} %get-tuple-element.8.gate_ref, s32[1,128]{1,0:T(1,128)} %get-tuple-element.9.slot_ref), custom_call_target="tpu_custom_call" | custom-call | tf_op jit(solution)/shard_map/pallas_call | solution.py:566

commit v5 on v4

--- a/solution.py
+++ b/solution.py
@@ -264,6 +264,12 @@
                 weight_loads[1].wait()
 
             project(c, 0, (0, 1))
+            pre_gate, pre_up = pre[0], pre[1]
+            sigmoid_gate = jax.nn.sigmoid(pre_gate)
+            swish_gate = pre_gate * sigmoid_gate
+            pre[3] = (swish_gate * pre_up).astype(BF).astype(F32)
+            pre[0] = pre_up * sigmoid_gate * (1.0 + pre_gate * (1.0 - sigmoid_gate))
+            pre[1] = swish_gate
             return
 
         @pl.when(c == 0)
@@ -271,16 +277,11 @@
             weight_loads[2].wait()
 
         project(c, 1, (2,))
-        pre_gate, pre_up, d_hidden = pre[0], pre[1], pre[2]
-        sigmoid_gate = jax.nn.sigmoid(pre_gate)
-        swish_gate = pre_gate * sigmoid_gate
-        hidden = (swish_gate * pre_up).astype(BF).astype(F32)
-        gate_part = jnp.sum(hidden * d_hidden, axis=1, keepdims=True)
+        d_hidden = pre[2]
+        gate_part = jnp.sum(pre[3] * d_hidden, axis=1, keepdims=True)
         part[c, :, 0:LANES] = jnp.broadcast_to(gate_part, (MANY, LANES)).astype(BF)
-        d_gate = (
-            d_hidden * pre_up * sigmoid_gate * (1.0 + pre_gate * (1.0 - sigmoid_gate))
-        ).astype(BF)
-        d_up = (d_hidden * swish_gate).astype(BF)
+        d_gate = (d_hidden * pre[0]).astype(BF)
+        d_up = (d_hidden * pre[1]).astype(BF)
         grads[0] = d_gate
         grads[1] = d_up
 
@@ -293,12 +294,13 @@
             ).astype(BF)
             return carry
 
+        quarter = HALF // 2 // NTILE
         for t in range(2):
-            lax.fori_loop(
-                t * HALF // NTILE, (t + 1) * HALF // NTILE, unproject, 0
-            )
-            for kind in range(4):
-                scatter_copy(c, t, kind).start()
+            for side, kinds in ((0, (0, 3)), (1, (1, 2))):
+                first = (2 * t + side) * quarter
+                lax.fori_loop(first, first + quarter, unproject, 0)
+                for kind in kinds:
+                    scatter_copy(c, t, kind).start()
 
     def scatter_columns(t, side):
         start = LANES + t * HALF + side * HALF // 2
@@ -531,7 +533,7 @@
             pltpu.VMEM((PIECES, SLOTS, PSUB, LANES), BF),
             pltpu.VMEM((PIECES, SLOTS, PSUB, LANES), BF),
             pltpu.VMEM((2, CHUNKS, MANY, D), BF),
-            pltpu.VMEM((3, MANY, HID), F32),
+            pltpu.VMEM((4, MANY, HID), F32),
             pltpu.VMEM((2, MANY, HID), BF),
             pltpu.VMEM((CHUNKS, MANY, WIDE), BF),
             pltpu.VMEM((CHUNKS, ROWS, WIDE), BF),

time: 190 us -> 190 us (level)
  no operation moved by 1% of the time
where the time goes in v5:
time: 190 us
  Pallas kernels  189 us (99%)
    pallas_call x1, Pallas kernels, local(): pl.pallas_call(kernel, out_shape=(jax.ShapeDtypeStruct((SLOTS, D), BF), j...  186 us

profile of v5, /device:TPU:1, one launch (start us, length us, event | category | flops | bytes accessed | tf_op | source)
XLA Modules:
  0.0 189.5 jit_solution(550550319145865969)
XLA Ops:
  0.6 186.2 %shard_map.86 = (bf16[192,4096]{1,0:T(8,128)(2,1)}, f32[1,128]{1,0:T(1,128)}, s32[1,128]{1,0:T(1,128)}) custom-call(bf16[128,4096]{1,0:T(8,128)(2,1)} %tok_hbm.1, bf16[128,4096]{1,0:T(8,128)(2,1)} %cot_hbm.1, s32[1,128]{1,0:T(1,128)} %bitcast.3, bf16[1,128]{1,0:T(2,128)(2,1)} %bitcast.4, bf16[1,384,4096]{2,1,0:T(8,128)(2,1)} %wg_hbm.1, ...), custom_call_target="tpu_custom_call" | custom-call | tf_op jit(solution)/shard_map/pallas_call | solution.py:521
  186.8 2.7 %shard_map.87 = (bf16[128,4096]{1,0:T(8,128)(2,1)}, bf16[1,128]{1,0:T(2,128)(2,1)}) custom-call(bf16[192,4096]{1,0:T(8,128)(2,1)} %get-tuple-element.7.home_ref, f32[1,128]{1,0:T(1,128)} %get-tuple-element.8.gate_ref, s32[1,128]{1,0:T(1,128)} %get-tuple-element.9.slot_ref), custom_call_target="tpu_custom_call" | custom-call | tf_op jit(solution)/shard_map/pallas_call | solution.py:568
